TPU v7x, 256 devices: a whole 4x4x8 slice. The times are simulated.
256 devices in a mesh: wide: 64 (over x, z, y_hi), narrow: 4 (over y_lo, core).
Axes of the slice: x: 4, y: 4 (y_hi: 2, y_lo: 2; y = y_hi * 2 + y_lo), z: 8, core: 2. Of those that a mesh axis runs over, the one named last changes fastest.
Arguments:
- images: bfloat16 [1024, 14, 14, 1024], P(('wide', 'narrow')), may hold values from -6 to 6
- dw_weight: float32 [7, 7, 1024], replicated, may hold values from -0.875 to 0.875
- dw_bias: float32 [1024], replicated, may hold values from -3 to 3
- ln_gain: float32 [1024], replicated, may hold values from 0.25 to 1.75
- ln_bias: float32 [1024], replicated, may hold values from -3 to 3
- w_in: bfloat16 [1024, 2048], P(None, ('wide', 'narrow')), may hold values from -0.1875 to 0.1875
- b_in: bfloat16 [2048], P(('wide', 'narrow')), may hold values from -3 to 3
- gamma: float32 [512], replicated, may hold values from 0.3 to 1
- curv_root: float32 [1024, 14, 14, 512], P(('wide', 'narrow')), may hold values from -24 to 24
- directions: float32 [2048, 1, 512], P(('wide', 'narrow')), may hold values from -30 to 30
Outputs:
- estimate: float32 [2048, 1, 512], P(('wide', 'narrow'))
All inputs are finite; a program needn't handle non-finite values.
Results may differ from a plain program's by a relative error of at most 0.0032.
Values may be sent and summed in bfloat16 or wider, within the bound.
A program may use at most 64 MiB of HBM per device.

v0:
```python
import jax
import jax.numpy as jnp
from jax import lax
from jax.sharding import PartitionSpec as P

damping = 0.05
scale_coef = 0.4
clip_ratio = 1.2


def centre(values, axis):
    return values - jnp.mean(values, axis=axis, keepdims=True)


def features(images, dw_weight, dw_bias, ln_gain, ln_bias):
    channels = images.shape[3]
    kernel = dw_weight.reshape(dw_weight.shape[0], dw_weight.shape[1], 1, channels)
    mixed = (
        lax.conv_general_dilated(
            images.astype(jnp.float32),
            kernel,
            (1, 1),
            "SAME",
            dimension_numbers=("NHWC", "HWIO", "NHWC"),
            feature_group_count=channels,
            precision=lax.Precision.HIGHEST,
        )
        + dw_bias
    )
    average = jnp.mean(mixed, axis=3, keepdims=True)
    variance = jnp.mean(jnp.square(mixed - average), axis=3, keepdims=True)
    normed = (mixed - average) * lax.rsqrt(variance + 1e-06) * ln_gain + ln_bias
    return normed.astype(jnp.bfloat16).reshape(images.shape[0], -1, channels)


def activate(normed, w_cols, b_cols):
    pre = jnp.einsum("ncd,dh->nch", normed, w_cols, preferred_element_type=jnp.float32) + b_cols[
        0
    ].astype(jnp.float32)
    return jax.nn.gelu(pre, approximate=False).astype(jnp.bfloat16)


def weights(cell_out, curvature, gamma):
    inner = curvature[:, None] * centre(cell_out, 2)
    return (centre(inner, 2) * (gamma * gamma)).astype(jnp.bfloat16)


def per_device(
    images, dw_weight, dw_bias, ln_gain, ln_bias, w_in, b_in, gamma, curv_root, directions
):
    own_images = images.shape[0]
    all_images = own_images * lax.axis_size("wide") * lax.axis_size("narrow")
    normed = features(images, dw_weight, dw_bias, ln_gain, ln_bias)
    cells = normed.shape[1]
    curvature = (0.25 + curv_root * curv_root).reshape(own_images, cells, -1)
    direction_sq = lax.psum(jnp.sum(directions * directions, axis=(0, 2)), ("wide", "narrow"))
    bias_row = b_in.reshape(1, -1)
    w_cols, b_cols = (
        lax.all_gather(w_in, ("wide", "narrow"), axis=1, tiled=True),
        lax.all_gather(bias_row, ("wide", "narrow"), axis=1, tiled=True),
    )
    hidden = activate(normed, w_cols, b_cols)
    estimate = directions
    rounded = estimate.astype(jnp.bfloat16)
    all_rows = lax.all_gather(rounded, ("wide", "narrow"), axis=0, tiled=True)
    cell_out = jnp.einsum("nch,hdk->ndck", hidden, all_rows, preferred_element_type=jnp.float32)
    cell_weight = weights(cell_out, curvature, gamma)
    product = lax.psum_scatter(
        jnp.einsum("nch,ndck->hdk", hidden, cell_weight, preferred_element_type=jnp.float32),
        ("wide", "narrow"),
        scatter_dimension=0,
        tiled=True,
    )
    fresh = directions + (1.0 - damping) * estimate - product / (scale_coef * all_images * cells)
    fresh_sq = lax.psum(jnp.sum(fresh * fresh, axis=(0, 2)), ("wide", "narrow"))
    factor = jnp.minimum(1.0, clip_ratio * jnp.sqrt(direction_sq / (fresh_sq + 1e-06)))
    estimate = fresh * factor[None, :, None]
    return estimate


def solution(mesh):
    placed = (
        P(("wide", "narrow"), None, None, None),
        P(),
        P(),
        P(),
        P(),
        P(None, ("wide", "narrow")),
        P(("wide", "narrow")),
        P(),
        P(("wide", "narrow"), None, None, None),
        P(("wide", "narrow"), None, None),
    )
    return jax.shard_map(
        per_device,
        mesh=mesh,
        in_specs=placed,
        out_specs=P(("wide", "narrow"), None, None),
        check_vma=False,
    )
```

profile of v0, /device:TPU:1, one launch (start us, length us, event | category | flops | bytes accessed | tf_op | source)
XLA Modules:
  0.0 1600.6 jit_solution(1470008976456797027)
XLA Ops:
  6.5 0.0 copy-start
  6.5 0.0 all-gather.4.cloned.1.call-start
  6.5 0.7 all-gather.4.cloned.1.call-update
  7.3 0.0 all-gather.6.cloned.1.call-start
  7.3 1.3 copy.41
  8.6 0.0 all-gather.6.cloned.1.call-update
  8.7 0.0 reduce-scatter.2.cloned.1.call-start
  8.7 0.0 copy-done
  8.7 0.0 copy-start.4
  8.7 0.0 copy-start.8
  8.7 18.7 %add_reduce_fusion = (f32[4,14,14]{0,2,1:T(8,128)S(1)}, f32[4,14,14,1024]{3,0,2,1:T(4,128)S(1)}) fusion(f32[1024]{0:T(1024)} %param.12, bf16[4,14,14,1024]{3,0,2,1:T(4,128)(2,1)S(1)} %copy-done, f32[7,7,1,1024]{3,1,0,2:T(8,128)} %bitcast.43), kind=kOutput, calls=%fused_computation.27 | convolution fusion | flops 365133056 | bytes 5024832 | tf_op jit(solution)/shard_map/conv_general_dilated | solution.py:19
  27.4 0.0 copy-start.1
  27.4 0.0 copy-start.5
  27.5 0.0 copy-start.6
  27.5 0.0 copy-start.7
  27.5 1.6 copy-done.1
  29.1 0.0 copy-done.4
  29.1 1.2 multiply_reduce_fusion
  30.4 0.0 copy-done.8
  30.4 0.2 dynamic-update-slice
  30.7 82.4 %all-reduce = bf16[2048]{0:T(1024)(128)(2,1)S(1)} all-reduce(bf16[2048]{0:T(1024)(128)(2,1)S(1)} %dynamic-update-slice), channel_id=2, replica_groups=mesh['wide'=64,'narrow'=4] {'wide','narrow'}, use_global_device_ids=true, to_apply=%add | all-reduce | flops 2048 | bytes 8192
  113.0 1.9 multiply_add_fusion
  114.9 0.0 copy-done.5
  114.9 0.0 copy-done.6
  115.0 0.0 copy-done.7
  115.0 3.8 add_convert_fusion
  118.8 11.6 all-gather.4.cloned.1.call-done
  130.4 8.5 fusion.16
  138.9 15.8 fusion.2
  154.7 80.8 %all-gather.6.cloned.1.call-done = bf16[2048,1,512]{2,0,1:T(8,128)(2,1)} async-done(((bf16[8,1,512]{2,0,1:T(8,128)(2,1)}), bf16[2048,1,512]{2,0,1:T(8,128)(2,1)}) %all-gather.6.cloned.1.call-update) | async-done | bytes 2097168 | tf_op jit(solution)/shard_map/all_gather | solution.py:65
  235.4 0.0 copy-start.2
  235.4 4.6 bitcast_reduce_fusion
  240.1 0.6 fusion.22
  240.7 0.0 copy-done.2
  240.7 0.0 copy-start.3
  240.7 4.5 convolution_bitcast_fusion
  245.2 0.0 reduce-scatter.2.cloned.1.call-update
  245.2 0.0 copy-done.3
  245.2 0.6 multiply_reduce_fusion.2
  245.9 1265.9 %reduce-scatter.2.cloned.1.call-done = f32[8,1,512]{2,0,1:T(8,128)} async-done(((f32[2048,1,512]{2,0,1:T(8,128)}), f32[8,1,512]{2,0,1:T(8,128)}) %reduce-scatter.2.cloned.1.call-update) | async-done | bytes 16400 | tf_op jit(solution)/shard_map/reduce_scatter | solution.py:68
  1511.8 1.4 multiply_reduce_fusion.1
  1513.2 78.2 %all-reduce.1 = (f32[1]{0:T(128)}, f32[1]{0:T(128)}) all-reduce(f32[1]{0:T(128)} %bitcast.14, f32[1]{0:T(128)} %bitcast.15), channel_id=1, replica_groups=mesh['wide'=64,'narrow'=4] {'wide','narrow'}, use_global_device_ids=true, to_apply=%region_6.0 | all-reduce | flops 2 | bytes 16 | tf_op jit(solution)/shard_map/psum | solution.py:56
  1592.7 0.7 broadcast_multiply_fusion.1
  1593.4 0.6 copy.24
  (7 shorter events, 0.1 us)
Async XLA Ops:
  6.5 2.2 copy-start
  6.5 123.9 %all-gather.4.cloned.1.call-start = ((), (), s32[]{:S(2)}) async-start(), calls=%async_computation.1 | async-start | bytes 4210688 | tf_op jit(solution)/shard_map/all_gather | solution.py:59
  7.3 228.2 %all-gather.6.cloned.1.call-start = ((), (), s32[]{:S(2)}) async-start(), calls=%async_computation.2 | async-start | bytes 2105344 | tf_op jit(solution)/shard_map/all_gather | solution.py:65
  8.7 1503.1 %reduce-scatter.2.cloned.1.call-start = ((), (), s32[]{:S(2)}) async-start(), calls=%async_computation.3 | async-start | bytes 4210688 | tf_op jit(solution)/shard_map/reduce_scatter | solution.py:68
  8.7 20.4 %copy-start.4 = (f32[1024]{0:T(1024)S(1)}, f32[1024]{0:T(1024)}, u32[]{:S(2)}) copy-start(f32[1024]{0:T(1024)} %param.12) | copy-start | bytes 12292
  8.7 21.7 %copy-start.8 = (bf16[8]{0:T(256)(128)(2,1)S(1)}, bf16[8]{0:T(256)(128)(2,1)}, u32[]{:S(2)}) copy-start(bf16[8]{0:T(256)(128)(2,1)} %param.16) | copy-start | bytes 52
  27.4 1.7 copy-start.1
  27.4 87.5 %copy-start.5 = (f32[512]{0:T(512)S(1)}, f32[512]{0:T(512)}, u32[]{:S(2)}) copy-start(f32[512]{0:T(512)} %param.17) | copy-start | bytes 6148
  27.5 87.5 %copy-start.6 = (f32[1024]{0:T(1024)S(1)}, f32[1024]{0:T(1024)}, u32[]{:S(2)}) copy-start(f32[1024]{0:T(1024)} %param.14) | copy-start | bytes 12292
  27.5 87.5 %copy-start.7 = (f32[1024]{0:T(1024)S(1)}, f32[1024]{0:T(1024)}, u32[]{:S(2)}) copy-start(f32[1024]{0:T(1024)} %param.13) | copy-start | bytes 12292
  235.4 5.2 copy-start.2
  240.7 4.5 copy-start.3
Sparse Core Ops, SparseCore 0:
  11.0 119.3 all-gather.3
  134.1 101.2 all-gather.5
  245.3 1266.3 reduce-scatter.1
where the time goes:
time: 1600 us
  waiting for transfers between devices  1360 us (85%)
  blocking collectives  161 us (10%)
  matrix products  36.2 us (2%)
  other arithmetic  26.1 us (2%)
    reduce_scatter x1, waiting for transfers between devices, per_device(): lax.psum_scatter(jnp.einsum('nch,ndck->hdk', hidden, cell_weight, preferr...  1270 us
    unnamed x1, blocking collectives  82.4 us
    all_gather x1, waiting for transfers between devices, per_device(): all_rows = lax.all_gather(rounded, ('wide', 'narrow'), axis=0, tiled=True)  80.8 us
    psum x1, blocking collectives, per_device(): lax.psum(jnp.sum(directions * directions, axis=(0, 2)), ('wide', 'narrow'))  78.2 us
  transfers between devices with their start and end apart: 3, of which 3 were waited for; matrix products, arithmetic and copies ran while one was open for 3% of the time, Pallas kernels for 0%

commit v1 on v0

v1 whole, which is shorter than its diff:
```python
import jax
import jax.numpy as jnp
from jax import lax
from jax.experimental import pallas as pl
from jax.experimental.pallas import tpu as pltpu
from jax.sharding import PartitionSpec as P

damping = 0.05
scale_coef = 0.4
clip_ratio = 1.2

MESH = pl.DeviceIdType.MESH
F32 = jnp.float32
BF16 = jnp.bfloat16

CH = 1024
HID = 2048
OUTC = 512
SIDE = 14
PAD = 16
IMGS = 4
CELLS = SIDE * SIDE
ROWS = IMGS * SIDE * PAD
ALL_CELLS = 1024 * CELLS
UNITS = 8
BLOCK = 64
WROWS = 8 * BLOCK + 16
DROWS = 4 * BLOCK
TILE = 256


def features(images, dw_weight, dw_bias, ln_gain, ln_bias):
    channels = images.shape[3]
    kernel = dw_weight.reshape(dw_weight.shape[0], dw_weight.shape[1], 1, channels)
    mixed = (
        lax.conv_general_dilated(
            images.astype(F32),
            kernel,
            (1, 1),
            "SAME",
            dimension_numbers=("NHWC", "HWIO", "NHWC"),
            feature_group_count=channels,
            precision=lax.Precision.HIGHEST,
        )
        + dw_bias
    )
    average = jnp.mean(mixed, axis=3, keepdims=True)
    variance = jnp.mean(jnp.square(mixed - average), axis=3, keepdims=True)
    normed = (mixed - average) * lax.rsqrt(variance + 1e-06) * ln_gain + ln_bias
    return normed.astype(BF16)


def gelu(pre):
    return 0.5 * pre * (1.0 + lax.erf(pre * 0.7071067811865476))


def body(
    normed_ref,
    wz_ref,
    gamma_ref,
    curv_ref,
    dir_ref,
    out_ref,
    wz,
    dz,
    wbuf,
    dbuf,
    hidden,
    cell_out,
    curvature,
    cell_weight,
    pair_send,
    pair_recv,
    slab_send,
    slab_recv,
    total,
    block_send,
    block_recv,
    row_send,
    row_recv,
    sums,
    sums_recv,
    wide_sums,
    wide_recv,
    send,
    recv,
):
    wide = lax.axis_index("wide")
    narrow = lax.axis_index("narrow")
    x = wide // 16
    z = (wide // 2) % 8
    y = (wide % 2) * 2 + narrow // 2
    c = narrow % 2
    a3 = x + c * (y - x)
    a2 = y + c * (x - y)

    def at(x_, y_, z_, c_):
        return ((x_ * 8 + z_) * 2 + y_ // 2, (y_ % 2) * 2 + c_)

    def along(a3_, a2_, z_):
        return at(a3_ + c * (a2_ - a3_), a2_ + c * (a3_ - a2_), z_, c)

    sibling = at(x, y, z, 1 - c)

    def group_of(k):
        spot = (z * 2 + c + k) % 16
        return at(x, y, spot // 2, spot % 2)

    def plane_of(k):
        spot = (x * 4 + y + k) % 16
        return at(spot // 4, spot % 4, z, c)

    def remote(src, dst, sem, device):
        return pltpu.make_async_remote_copy(
            src_ref=src,
            dst_ref=dst,
            send_sem=send.at[sem],
            recv_sem=recv.at[sem],
            device_id=device,
            device_id_type=MESH,
        )

    def arrived(sem, ref):
        pltpu.make_async_copy(ref, ref, recv.at[sem]).wait()

    def left(sem, ref):
        pltpu.make_async_copy(ref, ref, send.at[sem]).wait()

    barrier = pltpu.get_barrier_semaphore()
    for k in range(1, 16):
        pl.semaphore_signal(barrier, inc=1, device_id=group_of(k), device_id_type=MESH)
        pl.semaphore_signal(barrier, inc=1, device_id=plane_of(k), device_id_type=MESH)

    wz[z] = wz_ref[...]
    own = dir_ref[...]
    dz[z] = jnp.concatenate([own[:, :256], own[:, 256:]], axis=0).astype(BF16)

    pl.semaphore_wait(barrier, 30)

    def gather_z(buf, sem):
        for k in range(1, 8):
            remote(buf.at[z], buf.at[z], sem, along(a3, a2, (z + k) % 8)).start()

    def gather_a2(buf, sem):
        for k in range(1, 4):
            place = buf.at[c, a3, a2]
            remote(place, place, sem, along(a3, (a2 + k) % 4, z)).start()

    def slab(buf, off):
        return buf.at[c, (a3 + off) % 4]

    def to_sibling(buf, off, sem):
        remote(slab(buf, off), slab(buf, off), sem, sibling).start()

    def gather_a3(buf, sem):
        remote(slab(buf, 0), slab(buf, 0), sem, along((a3 + 1) % 4, a2, z)).start()
        remote(slab(buf, 0), slab(buf, 0), sem + 1, along((a3 + 3) % 4, a2, z)).start()
        to_sibling(buf, 0, sem + 4)

    def forward_low(buf, sem):
        arrived(sem, slab(buf, 3))
        part = buf.at[c, (a3 + 3) % 4, pl.ds(0, 2)]
        remote(part, part, sem + 2, along((a3 + 1) % 4, a2, z)).start()
        to_sibling(buf, 3, sem + 7)

    def forward_high(buf, sem):
        arrived(sem + 1, slab(buf, 1))
        part = buf.at[c, (a3 + 1) % 4, pl.ds(2, 2)]
        remote(part, part, sem + 3, along((a3 + 3) % 4, a2, z)).start()
        to_sibling(buf, 1, sem + 5)

    def forward_last(buf, sem):
        arrived(sem + 2, buf.at[c, (a3 + 2) % 4, pl.ds(0, 2)])
        arrived(sem + 3, buf.at[c, (a3 + 2) % 4, pl.ds(2, 2)])
        to_sibling(buf, 2, sem + 6)

    def slab_from_sibling(buf, off, sem):
        arrived(sem + 4 + off, buf.at[1 - c, (a2 + off) % 4])

    def drain(buf, zbuf, base):
        left(base, zbuf.at[pl.ds(0, 7)])
        left(base + 1, buf.at[0, 0, pl.ds(0, 3)])
        left(base + 2, buf.at[0, 0])
        left(base + 3, buf.at[0, 0])
        left(base + 4, buf.at[0, 0, pl.ds(0, 2)])
        left(base + 5, buf.at[0, 0, pl.ds(0, 2)])
        for off in range(4):
            left(base + 6 + off, buf.at[0, 0])

    def unpack_w():
        raw = wz[...].astype(F32)
        halves = (raw[:, :8, :512].reshape(BLOCK, 512), raw[:, 8:, :512].reshape(BLOCK, 512))
        for k in range(8):
            piece = halves[k // 4][:, (k % 4) * 128 : (k % 4 + 1) * 128]
            wbuf[c, a3, a2, pl.ds(k * BLOCK, BLOCK), :] = piece.astype(BF16)
        bias = raw[:, :8, 512:].reshape(BLOCK, 128)
        row_at = lax.broadcasted_iota(jnp.int32, (BLOCK, 128), 0)
        lane_at = lax.broadcasted_iota(jnp.int32, (BLOCK, 128), 1) % BLOCK
        line = jnp.sum(jnp.where(row_at == lane_at, bias, 0.0), axis=0, keepdims=True)
        wbuf[c, a3, a2, pl.ds(8 * BLOCK, 16), :] = jnp.broadcast_to(line, (16, 128)).astype(BF16)

    def unpack_d():
        raw = dz[...].astype(F32)
        halves = (raw[:, :8].reshape(BLOCK, 256), raw[:, 8:].reshape(BLOCK, 256))
        for k in range(4):
            piece = halves[k // 2][:, (k % 2) * 128 : (k % 2 + 1) * 128]
            dbuf[c, a3, a2, pl.ds(k * BLOCK, BLOCK), :] = piece.astype(BF16)

    order = [(0, 0), (1, 0), (0, 3), (1, 3), (0, 1), (1, 1), (0, 2), (1, 2)]

    def spot(p):
        half, off = order[p]
        if half == 0:
            return c, (a3 + off) % 4
        return 1 - c, (a2 + off) % 4

    def weight_tile(p):
        h, s = spot(p)
        return jnp.concatenate(
            [wbuf[h, s, :, k * BLOCK : (k + 1) * BLOCK, :].reshape(TILE, 128) for k in range(8)], axis=1
        )

    def bias_tile(p):
        h, s = spot(p)
        rows = wbuf[h, s, :, 8 * BLOCK :, :].astype(F32)
        lane = lax.broadcasted_iota(jnp.int32, (16, 128), 1)
        lines = [jnp.where(lane < BLOCK, rows[2 * k], rows[2 * k + 1])[:1] for k in range(2)]
        return jnp.concatenate(lines, axis=1)

    def direction_tile(p):
        h, s = spot(p)
        return jnp.concatenate(
            [dbuf[h, s, :, k * BLOCK : (k + 1) * BLOCK, :].reshape(TILE, 128) for k in range(4)], axis=1
        )

    W, D = 0, 10
    gather_z(wz, W)
    gather_z(dz, D)

    @pl.loop(0, IMGS)
    def _(i):
        root = curv_ref[i]
        curvature[i, :, 0:SIDE, :] = 0.25 + root * root
        curvature[i, :, SIDE:PAD, :] = jnp.zeros((SIDE, PAD - SIDE, OUTC), F32)

    arrived(W, wz.at[pl.ds(0, 7)])
    unpack_w()
    gather_a2(wbuf, W + 1)
    arrived(D, dz.at[pl.ds(0, 7)])
    unpack_d()
    gather_a2(dbuf, D + 1)
    arrived(W + 1, wbuf.at[0, 0, pl.ds(0, 3)])
    gather_a3(wbuf, W + 2)
    arrived(D + 1, dbuf.at[0, 0, pl.ds(0, 3)])
    forward_low(wbuf, W + 2)
    forward_high(wbuf, W + 2)
    gather_a3(dbuf, D + 2)

    def project(p):
        pre = lax.dot_general(
            normed_ref[...], weight_tile(p), (((1,), (1,)), ((), ())), preferred_element_type=F32
        )
        hidden[:, p * TILE : (p + 1) * TILE] = gelu(pre + bias_tile(p)).astype(BF16)

    project(0)
    slab_from_sibling(wbuf, 0, W + 2)
    project(1)
    forward_last(wbuf, W + 2)
    project(2)
    slab_from_sibling(wbuf, 3, W + 2)
    project(3)
    forward_low(dbuf, D + 2)
    forward_high(dbuf, D + 2)
    project(4)
    slab_from_sibling(wbuf, 1, W + 2)
    project(5)
    project(6)
    slab_from_sibling(wbuf, 2, W + 2)
    project(7)
    forward_last(dbuf, D + 2)
    for off in range(4):
        slab_from_sibling(dbuf, off, D + 2)

    directions = jnp.concatenate([direction_tile(p) for p in range(8)], axis=0)
    cell_out[...] = jnp.dot(hidden[...], directions, preferred_element_type=F32).reshape(
        IMGS, SIDE, PAD, OUTC
    )

    scale = gamma_ref[...] * gamma_ref[...]

    @pl.loop(0, IMGS)
    def _(i):
        inside = lax.broadcasted_iota(jnp.int32, (SIDE, PAD, OUTC), 1) < SIDE
        values = jnp.where(inside, cell_out[i], 0.0)
        mean = jnp.sum(values, axis=(0, 1), keepdims=True) * (1.0 / CELLS)
        inner = curvature[i] * (values - mean)
        again = jnp.sum(inner, axis=(0, 1), keepdims=True) * (1.0 / CELLS)
        final = jnp.where(inside, (inner - again) * scale[None], 0.0)
        cell_weight[i] = final.astype(BF16)

    def product(p):
        return lax.dot_general(
            hidden[:, p * TILE : (p + 1) * TILE],
            cell_weight[...].reshape(ROWS, OUTC),
            (((0,), (0,)), ((), ())),
            preferred_element_type=F32,
        )

    R = 20
    for off in (2, 1, 3, 0):
        pair_send[off] = product(order.index((1, off))).astype(BF16)
        remote(pair_send.at[off], pair_recv.at[off], R + off, sibling).start()
    for off in (2, 1, 3):
        part = product(order.index((0, off)))
        arrived(R + off, pair_recv.at[off])
        slab_send[off - 1] = (part + pair_recv[off].astype(F32)).astype(BF16)
        remote(
            slab_send.at[off - 1], slab_recv.at[off - 1], R + 3 + off, along((a3 + off) % 4, a2, z)
        ).start()
    part = product(order.index((0, 0)))
    arrived(R, pair_recv.at[0])
    part = part + pair_recv[0].astype(F32)
    for off in (1, 2, 3):
        arrived(R + 3 + off, slab_recv.at[off - 1])
        part = part + slab_recv[off - 1].astype(F32)
    total[...] = part.reshape(4, BLOCK, OUTC)
    for off in (2, 1, 3):
        block_send[off - 1] = total[(a2 + off) % 4].astype(BF16)
        remote(
            block_send.at[off - 1], block_recv.at[off - 1], R + 6 + off, along(a3, (a2 + off) % 4, z)
        ).start()
    part = total[a2]
    for off in (1, 2, 3):
        arrived(R + 6 + off, block_recv.at[off - 1])
        part = part + block_recv[off - 1].astype(F32)
    row_send[...] = part.reshape(8, UNITS, OUTC)
    for k in (4, 3, 5, 2, 6, 1, 7):
        remote(
            row_send.at[(z + k) % 8], row_recv.at[k - 1], R + 10, along(a3, a2, (z + k) % 8)
        ).start()
    arrived(R + 10, row_recv)
    summed = row_send[z] + jnp.sum(row_recv[...], axis=0)

    estimate = dir_ref[...]
    fresh = estimate + (1.0 - damping) * estimate - summed * (1.0 / (scale_coef * ALL_CELLS))
    fresh_part = jnp.sum(fresh * fresh, axis=(0, 1), keepdims=True)
    direction_part = jnp.sum(estimate * estimate, axis=(0, 1), keepdims=True)
    row = lax.broadcasted_iota(jnp.int32, (8, 128), 0)
    sums[...] = jnp.where(row < 4, fresh_part, direction_part)
    for k in range(1, 16):
        remote(sums, sums_recv.at[k - 1], R + 11, group_of(k)).start()
    arrived(R + 11, sums_recv)
    wide_sums[...] = sums[...] + jnp.sum(sums_recv[...], axis=0)
    for k in range(1, 16):
        remote(wide_sums, wide_recv.at[k - 1], R + 12, plane_of(k)).start()
    arrived(R + 12, wide_recv)
    sq = wide_sums[...] + jnp.sum(wide_recv[...], axis=0)
    fresh_sq = sq[0:1, 0:1]
    direction_sq = sq[4:5, 0:1]
    factor = jnp.minimum(1.0, clip_ratio * jnp.sqrt(direction_sq / (fresh_sq + 1e-06)))
    out_ref[...] = fresh * factor

    drain(wbuf, wz, W)
    drain(dbuf, dz, D)
    for off in range(4):
        left(R + off, pair_send.at[off])
    for off in range(1, 4):
        left(R + 3 + off, slab_send.at[off - 1])
        left(R + 6 + off, block_send.at[off - 1])
    left(R + 10, row_recv)
    left(R + 11, sums_recv)
    left(R + 12, wide_recv)


def step(normed, wz, gamma, curv_root, directions):
    vmem = pl.BlockSpec(memory_space=pltpu.VMEM)
    return pl.pallas_call(
        body,
        out_shape=jax.ShapeDtypeStruct((UNITS, OUTC), F32),
        in_specs=[vmem] * 5,
        out_specs=vmem,
        scratch_shapes=[
            pltpu.VMEM((8, 16, 640), BF16),
            pltpu.VMEM((8, 16, 256), BF16),
            pltpu.VMEM((2, 4, 4, WROWS, 128), BF16),
            pltpu.VMEM((2, 4, 4, DROWS, 128), BF16),
            pltpu.VMEM((ROWS, HID), BF16),
            pltpu.VMEM((IMGS, SIDE, PAD, OUTC), F32),
            pltpu.VMEM((IMGS, SIDE, PAD, OUTC), F32),
            pltpu.VMEM((IMGS, SIDE, PAD, OUTC), BF16),
            pltpu.VMEM((4, TILE, OUTC), BF16),
            pltpu.VMEM((4, TILE, OUTC), BF16),
            pltpu.VMEM((3, TILE, OUTC), BF16),
            pltpu.VMEM((3, TILE, OUTC), BF16),
            pltpu.VMEM((4, BLOCK, OUTC), F32),
            pltpu.VMEM((3, BLOCK, OUTC), BF16),
            pltpu.VMEM((3, BLOCK, OUTC), BF16),
            pltpu.VMEM((8, UNITS, OUTC), F32),
            pltpu.VMEM((7, UNITS, OUTC), F32),
            pltpu.VMEM((8, 128), F32),
            pltpu.VMEM((15, 8, 128), F32),
            pltpu.VMEM((8, 128), F32),
            pltpu.VMEM((15, 8, 128), F32),
            pltpu.SemaphoreType.DMA((40,)),
            pltpu.SemaphoreType.DMA((40,)),
        ],
        compiler_params=pltpu.CompilerParams(
            collective_id=0, has_side_effects=True, vmem_limit_bytes=52 * 1024 * 1024
        ),
    )(normed, wz, gamma, curv_root, directions)


def per_device(
    images, dw_weight, dw_bias, ln_gain, ln_bias, w_in, b_in, gamma, curv_root, directions
):
    normed = features(images, dw_weight, dw_bias, ln_gain, ln_bias)
    normed = jnp.pad(normed, ((0, 0), (0, 0), (0, PAD - SIDE), (0, 0))).reshape(ROWS, CH)
    weights = w_in.T.reshape(UNITS, 2, 512).transpose(1, 0, 2).reshape(16, 512)
    bias = jnp.broadcast_to(b_in[None, :, None], (2, UNITS, 128)).reshape(16, 128)
    wz = jnp.concatenate([weights, bias], axis=1)
    out = step(normed, wz, gamma.reshape(1, OUTC), curv_root, directions.reshape(UNITS, OUTC))
    return out.reshape(UNITS, 1, OUTC)


def solution(mesh):
    placed = (
        P(("wide", "narrow"), None, None, None),
        P(),
        P(),
        P(),
        P(),
        P(None, ("wide", "narrow")),
        P(("wide", "narrow")),
        P(),
        P(("wide", "narrow"), None, None, None),
        P(("wide", "narrow"), None, None),
    )
    return jax.shard_map(
        per_device,
        mesh=mesh,
        in_specs=placed,
        out_specs=P(("wide", "narrow"), None, None),
        check_vma=False,
    )
```

time: 1600 us -> 110 us (0.07)
  waiting for transfers between devices: 1360 us -> 0 us
  blocking collectives: 161 us -> 0 us
  Pallas kernels: 0 us -> 82.5 us
  other arithmetic: 26.1 us -> 2.74 us
  matrix products: 36.2 us -> 18.7 us
    reduce_scatter x1 -> x0, waiting for transfers between devices: 1270 us -> none  [per_device(): lax.psum_scatter(jnp.einsum('nch,ndck->hdk', hidden, cell_weight, preferr...]
    all_gather x2 -> x0, waiting for transfers between devices: 92.4 us -> none  [the longest x1 80.8 us: per_device(): all_rows = lax.all_gather(rounded, ('wide', 'narrow'), axis=0, tiled=True)]
    pallas_call x0 -> x1, Pallas kernels: none -> 82.5 us  [step(): pl.pallas_call(body, out_shape=jax.ShapeDtypeStruct((UNITS, OUTC), F32),...]
    unnamed x1 -> x0, blocking collectives: 82.4 us -> none
    psum x1 -> x0, blocking collectives: 78.2 us -> none  [per_device(): lax.psum(jnp.sum(directions * directions, axis=(0, 2)), ('wide', 'narrow'))]
    convert_element_type x3 -> x1, other arithmetic: 19.6 us -> 1.5 us  [features(): return normed.astype(BF16)]
    dot_general x3 -> x0, matrix products: 17.6 us -> none  [the longest x1 8.47 us: activate(): jnp.einsum('ncd,dh->nch', normed, w_cols, preferred_element_type=jnp.floa...]
  transfers between devices with their start and end apart: 3 -> 0, of which waited for: 3 -> 0; matrix products, arithmetic and copies ran while one was open for 3% -> 0% of each run, Pallas kernels for 0% -> 0%
where the time goes in v1:
time: 110 us; the launch traced here: 109 us
  Pallas kernels  82.5 us (75%)
  matrix products  18.7 us (17%)
  local copies, waits for them, and re-layouts  5.38 us (5%)
  other arithmetic  2.74 us (2%)
    pallas_call x1, Pallas kernels, step(): pl.pallas_call(body, out_shape=jax.ShapeDtypeStruct((UNITS, OUTC), F32),...  82.5 us
    conv_general_dilated x1, matrix products, features(): lax.conv_general_dilated(images.astype(F32), kernel, (1, 1), 'SAME', dime...  18.7 us
    unnamed x21, local copies, waits for them, and re-layouts  4.29 us

profile of v1, /device:TPU:1, one launch (start us, length us, event | category | flops | bytes accessed | tf_op | source)
XLA Modules:
  0.0 109.4 jit_solution(7920556032319704506)
XLA Ops:
  0.0 0.0 copy-start
  0.0 1.4 %copy-done = bf16[4,14,14,1024]{3,0,2,1:T(4,128)(2,1)S(1)} copy-done((bf16[4,14,14,1024]{3,0,2,1:T(4,128)(2,1)S(1)}, bf16[4,14,14,1024]{3,0,2,1:T(4,128)(2,1)}, u32[]{:S(2)}) %copy-start) | copy-done | bytes 1605656
  1.4 0.0 copy-start.5
  1.4 18.7 %add_reduce_fusion = (f32[4,14,14]{0,2,1:T(8,128)S(1)}, f32[4,14,14,1024]{3,0,2,1:T(4,128)S(1)}) fusion(f32[1024]{0:T(1024)} %param.12, bf16[4,14,14,1024]{3,0,2,1:T(4,128)(2,1)S(1)} %copy-done, f32[7,7,1,1024]{3,1,0,2:T(8,128)} %bitcast.20), kind=kOutput, calls=%fused_computation.2 | convolution fusion | flops 365133056 | bytes 5024832 | tf_op jit(solution)/shard_map/conv_general_dilated | solution.py:36
  20.1 0.0 copy-start.6
  20.1 0.0 copy-start.7
  20.2 0.0 copy-done.5
  20.2 1.2 %multiply_reduce_fusion = f32[4,14,14]{0,2,1:T(8,128)S(1)} fusion(f32[4,14,14,1024]{3,0,2,1:T(4,128)S(1)} %get-tuple-element.6, f32[4,14,14]{0,2,1:T(8,128)S(1)} %broadcast_multiply_fusion, f32[1024]{0:T(1024)S(1)} %copy-done.5), kind=kLoop, calls=%fused_computation.1 | loop fusion | flops 3210480 | bytes 3221632 | tf_op jit(solution)/shard_map/reduce_sum | solution.py:48
  21.4 0.0 copy-done.6
  21.4 0.0 copy-done.7
  21.4 1.5 %add_convert_fusion = bf16[4,14,14,1024]{3,0,2,1:T(4,128)(2,1)S(1)} fusion(f32[4,14,14,1024]{3,0,2,1:T(4,128)S(1)} %get-tuple-element.6, f32[1024]{0:T(1024)S(1)} %copy-done.6, f32[1024]{0:T(1024)S(1)} %copy-done.7, f32[4,14,14]{0,2,1:T(8,128)S(1)} %add_rsqrt_fusion, f32[4,14,14]{0,2,1:T(8,128)S(1)} %broadcast_multiply_fusion, f32[1024]{0:T(1024)S(1)} %copy-done.5), kind=kLoop, calls=%fused_computation | loop fusion | flops 4816896 | bytes 4835456 | tf_op jit(solution)/shard_map/convert_element_type | solution.py:50
  22.9 0.0 copy-start.2
  22.9 0.5 copy.16
  23.5 0.0 copy-start.8
  23.5 0.0 copy-start.3
  23.5 0.0 copy-start.4
  23.5 0.0 copy-start.1
  23.5 0.3 pad.4.clone
  23.8 0.5 copy-done.2
  24.3 1.8 %copy.13.curv_ref = f32[4,14,14,512]{3,2,1,0:T(8,128)} copy(f32[4,14,14,512]{3,0,2,1:T(4,128)S(1)} %copy-done.2) | data formatting | bytes 3211264 | tf_op args[8]
  26.1 0.0 copy-done.8
  26.1 0.1 broadcast_in_dim.7
  26.2 0.1 broadcast_in_dim.8
  26.3 0.0 copy-done.3
  26.3 0.0 copy-done.4
  26.3 0.0 copy-done.1
  26.3 82.5 %shard_map.100 = f32[8,512]{1,0:T(8,128)S(1)} custom-call(bf16[896,1024]{1,0:T(8,128)(2,1)S(1)} %bitcast.15, bf16[16,640]{1,0:T(8,128)(2,1)S(1)} %pad_maximum_fusion.wz_ref, f32[1,512]{1,0:T(1,128)S(1)} %bitcast.18, f32[4,14,14,512]{3,2,1,0:T(8,128)} %copy.13.curv_ref, f32[8,512]{1,0:T(8,128)S(1)} %bitcast.17), custom_call_target="tpu_custom_call" | custom-call | tf_op jit(solution)/shard_map/pallas_call | solution.py:377
  108.8 0.6 copy.14
  (5 shorter events, 0.0 us)
Async XLA Ops:
  0.0 1.4 %copy-start = (bf16[4,14,14,1024]{3,0,2,1:T(4,128)(2,1)S(1)}, bf16[4,14,14,1024]{3,0,2,1:T(4,128)(2,1)}, u32[]{:S(2)}) copy-start(bf16[4,14,14,1024]{3,0,2,1:T(4,128)(2,1)} %param.10) | copy-start | bytes 4816900
  1.4 18.7 %copy-start.5 = (f32[1024]{0:T(1024)S(1)}, f32[1024]{0:T(1024)}, u32[]{:S(2)}) copy-start(f32[1024]{0:T(1024)} %param.12) | copy-start | bytes 12292
  20.1 1.3 %copy-start.6 = (f32[1024]{0:T(1024)S(1)}, f32[1024]{0:T(1024)}, u32[]{:S(2)}) copy-start(f32[1024]{0:T(1024)} %param.14) | copy-start | bytes 12292
  20.1 1.3 %copy-start.7 = (f32[1024]{0:T(1024)S(1)}, f32[1024]{0:T(1024)}, u32[]{:S(2)}) copy-start(f32[1024]{0:T(1024)} %param.13) | copy-start | bytes 12292
  22.9 1.4 %copy-start.2 = (f32[4,14,14,512]{3,0,2,1:T(4,128)S(1)}, f32[4,14,14,512]{3,0,2,1:T(4,128)}, u32[]{:S(2)}) copy-start(f32[4,14,14,512]{3,0,2,1:T(4,128)} %param.18) | copy-start | bytes 4816900
  23.5 2.7 %copy-start.8 = (bf16[8]{0:T(256)(128)(2,1)S(1)}, bf16[8]{0:T(256)(128)(2,1)}, u32[]{:S(2)}) copy-start(bf16[8]{0:T(256)(128)(2,1)} %param.16) | copy-start | bytes 52
  23.5 2.8 %copy-start.3 = (bf16[1024,8]{0,1:T(8,128)(2,1)S(1)}, bf16[1024,8]{0,1:T(8,128)(2,1)}, u32[]{:S(2)}) copy-start(bf16[1024,8]{0,1:T(8,128)(2,1)} %param.15) | copy-start | bytes 49156
  23.5 2.8 %copy-start.4 = (f32[8,1,512]{2,1,0:T(1,128)S(1)}, f32[8,1,512]{2,1,0:T(1,128)}, u32[]{:S(2)}) copy-start(f32[8,1,512]{2,1,0:T(1,128)} %param.19) | copy-start | bytes 49156
  23.5 2.8 %copy-start.1 = (f32[512]{0:T(512)S(1)}, f32[512]{0:T(512)}, u32[]{:S(2)}) copy-start(f32[512]{0:T(512)} %param.17) | copy-start | bytes 6148

commit v2 on v1

v2 whole, which is shorter than its diff:
```python
import jax
import jax.numpy as jnp
from jax import lax
from jax.experimental import pallas as pl
from jax.experimental.pallas import tpu as pltpu
from jax.sharding import PartitionSpec as P

damping = 0.05
scale_coef = 0.4
clip_ratio = 1.2

MESH = pl.DeviceIdType.MESH
F32 = jnp.float32
BF16 = jnp.bfloat16

CH = 1024
HID = 2048
OUTC = 512
SIDE = 14
KER = 7
IMGS = 4
CELLS = SIDE * SIDE
ROWS = IMGS * CELLS
ALL_CELLS = 1024 * CELLS
UNITS = 8
BLOCK = 64
WROWS = 8 * BLOCK + 16
DROWS = 4 * BLOCK
TILE = 256
PAIR = 2 * SIDE


def gelu(pre):
    return 0.5 * pre * (1.0 + lax.erf(pre * 0.7071067811865476))


def low_rows(shape):
    return lax.broadcasted_iota(jnp.int32, shape, len(shape) - 2) < 4


def folded(values):
    return values + pltpu.roll(values, 4, values.ndim - 2)


def unzip(values):
    count = values.shape[0] // 2
    pairs = values.reshape(count, 2, 8, 128)
    even, odd = pairs[:, 0], pairs[:, 1]
    low = low_rows((count, 8, 128))
    return (
        jnp.where(low, even, pltpu.roll(odd, 4, 1)),
        jnp.where(low, pltpu.roll(even, 4, 1), odd),
    )


def body(
    images_hbm,
    kernel_hbm,
    dw_bias_ref,
    gain_ref,
    ln_bias_ref,
    w_ref,
    b_ref,
    gamma_ref,
    curv_hbm,
    dir_ref,
    out_ref,
    images,
    kernel,
    roots,
    pixels,
    taps,
    scales,
    mixed,
    normed,
    curvature,
    wz,
    dz,
    wbuf,
    dbuf,
    hidden,
    cell_out,
    cell_weight,
    pair_send,
    pair_recv,
    slab_send,
    slab_recv,
    block_send,
    block_recv,
    row_send,
    row_recv,
    sums,
    sums_recv,
    wide_sums,
    wide_recv,
    send,
    recv,
    load,
):
    loads = [
        pltpu.make_async_copy(images_hbm, images, load.at[0]),
        pltpu.make_async_copy(kernel_hbm, kernel, load.at[1]),
        pltpu.make_async_copy(curv_hbm, roots, load.at[2]),
    ]
    for copy in loads:
        copy.start()

    wide = lax.axis_index("wide")
    narrow = lax.axis_index("narrow")
    x = wide // 16
    z = (wide // 2) % 8
    y = (wide % 2) * 2 + narrow // 2
    c = narrow % 2
    a3 = x + c * (y - x)
    a2 = y + c * (x - y)

    def at(x_, y_, z_, c_):
        return ((x_ * 8 + z_) * 2 + y_ // 2, (y_ % 2) * 2 + c_)

    def along(k3, k2, kz):
        a3_ = (a3 + k3) % 4
        a2_ = (a2 + k2) % 4
        return at(a3_ + c * (a2_ - a3_), a2_ + c * (a3_ - a2_), (z + kz) % 8, c)

    sibling = at(x, y, z, 1 - c)

    def group_of(k):
        spot = (z * 2 + c + k) % 16
        return at(x, y, spot // 2, spot % 2)

    def plane_of(k):
        spot = (x * 4 + y + k) % 16
        return at(spot // 4, spot % 4, z, c)

    def remote(src, dst, sem, device):
        return pltpu.make_async_remote_copy(
            src_ref=src,
            dst_ref=dst,
            send_sem=send.at[sem],
            recv_sem=recv.at[sem],
            device_id=device,
            device_id_type=MESH,
        )

    def arrived(sem, ref):
        pltpu.make_async_copy(ref, ref, recv.at[sem]).wait()

    def left(sem, ref):
        pltpu.make_async_copy(ref, ref, send.at[sem]).wait()

    barrier = pltpu.get_barrier_semaphore()
    for k in range(1, 16):
        pl.semaphore_signal(barrier, inc=1, device_id=group_of(k), device_id_type=MESH)
        pl.semaphore_signal(barrier, inc=1, device_id=plane_of(k), device_id_type=MESH)

    wz[0, :, 0:512] = w_ref[...]
    row8 = lax.broadcasted_iota(jnp.int32, (8, 8), 0)
    lane8 = lax.broadcasted_iota(jnp.int32, (8, 8), 1)
    line = jnp.broadcast_to(b_ref[...].astype(F32), (8, 8))
    column = jnp.sum(jnp.where(row8 == lane8, line, 0.0), axis=1, keepdims=True)
    column = jnp.broadcast_to(column, (8, 128))
    wz[0, :, 512:640] = jnp.concatenate([column, column], axis=0).astype(BF16)
    own = dir_ref[...]
    dz[0] = jnp.concatenate([own[:, :256], own[:, 256:]], axis=0).astype(BF16)

    def gather_z(buf, sem):
        for k in range(1, 8):
            remote(buf.at[0], buf.at[8 - k], sem, along(0, 0, k)).start()

    def gather_a2(buf, sem):
        for k in range(1, 4):
            remote(buf.at[0, 0, 0], buf.at[0, 0, 4 - k], sem, along(0, k, 0)).start()

    def spread(buf, k, lo, count, sem):
        part = pl.ds(lo, count)
        remote(buf.at[0, 0, part], buf.at[0, 4 - k, part], sem, along(k, 0, 0)).start()

    def to_sibling(buf, off, sem):
        remote(buf.at[0, off], buf.at[1, off], sem, sibling).start()

    def unpack_w():
        raw = wz[...].astype(F32)
        halves = (raw[:, :8, :512].reshape(BLOCK, 512), raw[:, 8:, :512].reshape(BLOCK, 512))
        for k in range(8):
            piece = halves[k // 4][:, (k % 4) * 128 : (k % 4 + 1) * 128]
            wbuf[0, 0, 0, k * BLOCK : (k + 1) * BLOCK, :] = piece.astype(BF16)
        bias = raw[:, :8, 512:].reshape(BLOCK, 128)
        row_at = lax.broadcasted_iota(jnp.int32, (BLOCK, 128), 0)
        lane_at = lax.broadcasted_iota(jnp.int32, (BLOCK, 128), 1) % BLOCK
        total = jnp.sum(jnp.where(row_at == lane_at, bias, 0.0), axis=0, keepdims=True)
        wbuf[0, 0, 0, 8 * BLOCK :, :] = jnp.broadcast_to(total, (16, 128)).astype(BF16)

    def unpack_d():
        raw = dz[...].astype(F32)
        halves = (raw[:, :8].reshape(BLOCK, 256), raw[:, 8:].reshape(BLOCK, 256))
        for k in range(4):
            piece = halves[k // 2][:, (k % 2) * 128 : (k % 2 + 1) * 128]
            dbuf[0, 0, 0, k * BLOCK : (k + 1) * BLOCK, :] = piece.astype(BF16)

    def weight_tile(h, s):
        return jnp.concatenate(
            [wbuf[h, s, :, k * BLOCK : (k + 1) * BLOCK, :].reshape(TILE, 128) for k in range(8)], axis=1
        )

    def bias_tile(h, s):
        rows = wbuf[h, s, :, 8 * BLOCK :, :].astype(F32)
        lane = lax.broadcasted_iota(jnp.int32, (16, 128), 1)
        lines = [jnp.where(lane < BLOCK, rows[2 * k], rows[2 * k + 1])[:1] for k in range(2)]
        return jnp.concatenate(lines, axis=1)

    def direction_tile(h, s):
        return jnp.concatenate(
            [dbuf[h, s, :, k * BLOCK : (k + 1) * BLOCK, :].reshape(TILE, 128) for k in range(4)], axis=1
        )

    def two_tiles(row, j):
        return jnp.where(
            low_rows((8, 128)),
            jnp.broadcast_to(row[:, 2 * j * 128 : (2 * j + 1) * 128], (8, 128)),
            jnp.broadcast_to(row[:, (2 * j + 1) * 128 : (2 * j + 2) * 128], (8, 128)),
        )

    def conv_rows(first):
        @pl.loop(0, 4)
        def _(j):
            for r in (first, first + 1):
                acc = [None] * SIDE
                for kh in range(KER):
                    source = r + kh - KER // 2
                    if source < 0 or source >= SIDE:
                        continue
                    line = [taps[j, kh * KER + kw] for kw in range(KER)]
                    for col in range(SIDE):
                        value = pixels[j, source * SIDE + col]
                        for kw in range(KER):
                            to = col - kw + KER // 2
                            if 0 <= to < SIDE:
                                term = value * line[kw]
                                acc[to] = term if acc[to] is None else acc[to] + term
                shift = scales[0, j]
                for col in range(SIDE):
                    mixed[j, (r - first) * SIDE + col] = acc[col] + shift

    def norm_rows(first):
        parts = [mixed[j] for j in range(4)]
        total = jnp.sum(folded(parts[0] + parts[1] + parts[2] + parts[3]), axis=2, keepdims=True)
        average = total * (1.0 / CH)
        parts = [part - average for part in parts]
        squares = [part * part for part in parts]
        total = jnp.sum(folded(squares[0] + squares[1] + squares[2] + squares[3]), axis=2, keepdims=True)
        rstd = lax.rsqrt(total * (1.0 / CH) + 1e-06)
        lo = first * SIDE * IMGS
        for j in range(4):
            values = unzip(parts[j] * rstd * scales[1, j] + scales[2, j])
            for k in range(2):
                lane = (2 * j + k) * 128
                normed[lo : lo + PAIR * IMGS, lane : lane + 128] = (
                    values[k].reshape(PAIR * IMGS, 128).astype(BF16)
                )

    loads[1].wait()

    @pl.loop(0, KER)
    def _(kh):
        for kw in range(KER):
            line = kernel[kh, kw : kw + 1, :]
            for j in range(4):
                taps[j, kh * KER + kw] = two_tiles(line, j)

    for j in range(4):
        scales[0, j] = two_tiles(dw_bias_ref[...], j)
        scales[1, j] = two_tiles(gain_ref[...], j)
        scales[2, j] = two_tiles(ln_bias_ref[...], j)

    loads[0].wait()

    @pl.loop(0, SIDE)
    def _(r):
        cells = pl.ds(r * SIDE, SIDE)
        for j in range(2):
            block = images[cells, 16 * j : 16 * j + 16, :].astype(F32)
            pixels[2 * j, cells] = block[:, :8]
            pixels[2 * j + 1, cells] = block[:, 8:]

    W, D = 0, 20
    pl.semaphore_wait(barrier, 30)
    gather_z(wz, W)
    gather_z(dz, D)

    def conv(first):
        conv_rows(first)
        norm_rows(first)

    conv(0)
    conv(2)
    conv(4)

    arrived(W, wz.at[pl.ds(1, 7)])
    unpack_w()
    gather_a2(wbuf, W + 1)
    spread(wbuf, 1, 0, 1, W + 2)
    spread(wbuf, 3, 0, 1, W + 3)
    arrived(D, dz.at[pl.ds(1, 7)])
    unpack_d()
    gather_a2(dbuf, D + 1)

    conv(6)
    conv(8)

    arrived(W + 1, wbuf.at[0, 0, pl.ds(1, 3)])
    spread(wbuf, 1, 1, 3, W + 4)
    spread(wbuf, 3, 1, 3, W + 5)
    to_sibling(wbuf, 0, W + 6)

    conv(10)

    arrived(D + 1, dbuf.at[0, 0, pl.ds(1, 3)])
    to_sibling(dbuf, 0, D + 6)

    conv(12)

    for k in (1, 3, 2):
        spread(dbuf, k, 0, 4, D + 1 + k)

    def project(p, h, s):
        pre = lax.dot_general(
            normed[...], weight_tile(h, s), (((1,), (1,)), ((), ())), preferred_element_type=F32
        )
        hidden[:, p * TILE : (p + 1) * TILE] = gelu(pre + bias_tile(h, s)).astype(BF16)

    places = [(0, 0), (1, 0), (0, 3), (1, 3), (0, 1), (1, 1), (0, 2), (1, 2)]

    project(0, 0, 0)
    arrived(W + 6, wbuf.at[1, 0])
    project(1, 1, 0)

    loads[2].wait()
    for k in range(2):
        root = roots[:, 8 * k : 8 * k + 8, :]
        first, second = unzip(0.25 + root * root)
        curvature[2 * k] = first
        curvature[2 * k + 1] = second

    arrived(W + 2, wbuf.at[0, 3, pl.ds(0, 1)])
    arrived(W + 4, wbuf.at[0, 3, pl.ds(1, 3)])
    remote(wbuf.at[0, 3, pl.ds(0, 2)], wbuf.at[0, 2, pl.ds(0, 2)], W + 10, along(1, 0, 0)).start()
    to_sibling(wbuf, 3, W + 9)
    arrived(W + 3, wbuf.at[0, 1, pl.ds(0, 1)])
    arrived(W + 5, wbuf.at[0, 1, pl.ds(1, 3)])
    remote(wbuf.at[0, 1, pl.ds(2, 2)], wbuf.at[0, 2, pl.ds(2, 2)], W + 11, along(3, 0, 0)).start()
    to_sibling(wbuf, 1, W + 7)
    project(2, 0, 3)
    arrived(W + 9, wbuf.at[1, 3])
    project(3, 1, 3)
    project(4, 0, 1)
    arrived(W + 7, wbuf.at[1, 1])
    project(5, 1, 1)
    arrived(W + 10, wbuf.at[0, 2, pl.ds(0, 2)])
    arrived(W + 11, wbuf.at[0, 2, pl.ds(2, 2)])
    to_sibling(wbuf, 2, W + 8)
    project(6, 0, 2)
    for k in (1, 3, 2):
        arrived(D + 1 + k, dbuf.at[0, 4 - k])
        to_sibling(dbuf, 4 - k, D + 6 + 4 - k)
    arrived(W + 8, wbuf.at[1, 2])
    project(7, 1, 2)
    for off in range(4):
        arrived(D + 6 + off, dbuf.at[1, off])

    directions = jnp.concatenate([direction_tile(h, s) for h, s in places], axis=0)
    cell_out[...] = jnp.dot(hidden[...], directions, preferred_element_type=F32)

    scale = gamma_ref[...] * gamma_ref[...]
    for k in range(4):
        lanes = slice(k * 128, (k + 1) * 128)
        values = cell_out[:, lanes].reshape(CELLS // 2, 8, 128)
        mean = folded(jnp.sum(values, axis=0)) * (1.0 / CELLS)
        inner = curvature[k] * (values - mean)
        again = folded(jnp.sum(inner, axis=0)) * (1.0 / CELLS)
        final = (inner - again) * scale[:, lanes]
        cell_weight[:, lanes] = final.reshape(ROWS, 128).astype(BF16)

    def product(h, s):
        p = places.index((h, s))
        return lax.dot_general(
            hidden[:, p * TILE : (p + 1) * TILE],
            cell_weight[...],
            (((0,), (0,)), ((), ())),
            preferred_element_type=F32,
        )

    R = 40
    for off in (2, 1, 3, 0):
        pair_send[off] = product(1, off).astype(BF16)
        remote(pair_send.at[off], pair_recv.at[off], R + off, sibling).start()
    for off in (2, 1, 3):
        part = product(0, off)
        arrived(R + off, pair_recv.at[off])
        slab_send[off - 1] = (part + pair_recv[off].astype(F32)).astype(BF16)
        remote(slab_send.at[off - 1], slab_recv.at[off - 1], R + 3 + off, along(off, 0, 0)).start()
    part = product(0, 0)
    arrived(R, pair_recv.at[0])
    part = part + pair_recv[0].astype(F32)
    for off in (1, 3, 2):
        arrived(R + 3 + off, slab_recv.at[off - 1])
        part = part + slab_recv[off - 1].astype(F32)
    blocks = part.reshape(4, BLOCK, OUTC)
    for off in (2, 1, 3):
        block_send[off - 1] = blocks[off].astype(BF16)
        remote(block_send.at[off - 1], block_recv.at[off - 1], R + 6 + off, along(0, off, 0)).start()
    part = blocks[0]
    for off in (1, 3, 2):
        arrived(R + 6 + off, block_recv.at[off - 1])
        part = part + block_recv[off - 1].astype(F32)
    rows = part.reshape(8, UNITS, OUTC)
    for k in (4, 3, 5, 2, 6, 1, 7):
        row_send[k - 1] = jnp.concatenate([rows[k, :, :256], rows[k, :, 256:]], axis=0).astype(BF16)
        remote(row_send.at[k - 1], row_recv.at[k - 1], R + 10, along(0, 0, k)).start()
    arrived(R + 10, row_recv)
    others = jnp.sum(row_recv[...].astype(F32), axis=0)
    summed = rows[0] + jnp.concatenate([others[:8], others[8:]], axis=1)

    estimate = dir_ref[...]
    fresh = estimate + (1.0 - damping) * estimate - summed * (1.0 / (scale_coef * ALL_CELLS))
    fresh_part = jnp.sum(fresh * fresh, axis=(0, 1), keepdims=True)
    direction_part = jnp.sum(estimate * estimate, axis=(0, 1), keepdims=True)
    row = lax.broadcasted_iota(jnp.int32, (8, 128), 0)
    sums[...] = jnp.where(row < 4, fresh_part, direction_part)
    for k in range(1, 16):
        remote(sums, sums_recv.at[k - 1], R + 11, group_of(k)).start()
    arrived(R + 11, sums_recv)
    wide_sums[...] = sums[...] + jnp.sum(sums_recv[...], axis=0)
    for k in range(1, 16):
        remote(wide_sums, wide_recv.at[k - 1], R + 12, plane_of(k)).start()
    arrived(R + 12, wide_recv)
    sq = wide_sums[...] + jnp.sum(wide_recv[...], axis=0)
    fresh_sq = sq[0:1, 0:1]
    direction_sq = sq[4:5, 0:1]
    factor = jnp.minimum(1.0, clip_ratio * jnp.sqrt(direction_sq / (fresh_sq + 1e-06)))
    out_ref[...] = fresh * factor

    for buf, zbuf, base in ((wbuf, wz, W), (dbuf, dz, D)):
        left(base, zbuf.at[pl.ds(1, 7)])
        left(base + 1, buf.at[0, 0, pl.ds(1, 3)])
        for off in range(4):
            left(base + 6 + off, buf.at[0, off])
    for k in range(2):
        left(W + 2 + k, wbuf.at[0, 0, pl.ds(0, 1)])
        left(W + 4 + k, wbuf.at[0, 0, pl.ds(1, 3)])
        left(W + 10 + k, wbuf.at[0, 0, pl.ds(0, 2)])
    for k in (1, 3, 2):
        left(D + 1 + k, dbuf.at[0, 0])
    for off in range(4):
        left(R + off, pair_send.at[off])
    for off in range(1, 4):
        left(R + 3 + off, slab_send.at[off - 1])
        left(R + 6 + off, block_send.at[off - 1])
    left(R + 10, row_recv)
    left(R + 11, sums_recv)
    left(R + 12, wide_recv)


def step(*operands):
    vmem = pl.BlockSpec(memory_space=pltpu.VMEM)
    hbm = pl.BlockSpec(memory_space=pl.ANY)
    return pl.pallas_call(
        body,
        out_shape=jax.ShapeDtypeStruct((UNITS, OUTC), F32),
        in_specs=[hbm, hbm, vmem, vmem, vmem, vmem, vmem, vmem, hbm, vmem],
        out_specs=vmem,
        scratch_shapes=[
            pltpu.VMEM((CELLS, 32, 128), BF16),
            pltpu.VMEM((KER, KER, CH), F32),
            pltpu.VMEM((CELLS, 16, 128), F32),
            pltpu.VMEM((4, CELLS, 8, 128), F32),
            pltpu.VMEM((4, KER * KER, 8, 128), F32),
            pltpu.VMEM((3, 4, 8, 128), F32),
            pltpu.VMEM((4, PAIR, 8, 128), F32),
            pltpu.VMEM((ROWS, CH), BF16),
            pltpu.VMEM((4, CELLS // 2, 8, 128), F32),
            pltpu.VMEM((8, 16, 640), BF16),
            pltpu.VMEM((8, 16, 256), BF16),
            pltpu.VMEM((2, 4, 4, WROWS, 128), BF16),
            pltpu.VMEM((2, 4, 4, DROWS, 128), BF16),
            pltpu.VMEM((ROWS, HID), BF16),
            pltpu.VMEM((ROWS, OUTC), F32),
            pltpu.VMEM((ROWS, OUTC), BF16),
            pltpu.VMEM((4, TILE, OUTC), BF16),
            pltpu.VMEM((4, TILE, OUTC), BF16),
            pltpu.VMEM((3, TILE, OUTC), BF16),
            pltpu.VMEM((3, TILE, OUTC), BF16),
            pltpu.VMEM((3, BLOCK, OUTC), BF16),
            pltpu.VMEM((3, BLOCK, OUTC), BF16),
            pltpu.VMEM((7, 16, 256), BF16),
            pltpu.VMEM((7, 16, 256), BF16),
            pltpu.VMEM((8, 128), F32),
            pltpu.VMEM((15, 8, 128), F32),
            pltpu.VMEM((8, 128), F32),
            pltpu.VMEM((15, 8, 128), F32),
            pltpu.SemaphoreType.DMA((60,)),
            pltpu.SemaphoreType.DMA((60,)),
            pltpu.SemaphoreType.DMA((3,)),
        ],
        compiler_params=pltpu.CompilerParams(
            collective_id=0, has_side_effects=True, vmem_limit_bytes=56 * 1024 * 1024
        ),
    )(*operands)


def cell_major(array):
    tiles = array.shape[3] // 128
    cells = array.transpose(1, 2, 0, 3).reshape(CELLS, IMGS, tiles, 128)
    return cells.transpose(0, 2, 1, 3).reshape(CELLS, tiles * IMGS, 128)


def per_device(
    images, dw_weight, dw_bias, ln_gain, ln_bias, w_in, b_in, gamma, curv_root, directions
):
    out = step(
        cell_major(images),
        dw_weight,
        dw_bias.reshape(1, CH),
        ln_gain.reshape(1, CH),
        ln_bias.reshape(1, CH),
        w_in.T.reshape(UNITS, 2, 512).transpose(1, 0, 2).reshape(16, 512),
        b_in.reshape(1, UNITS),
        gamma.reshape(1, OUTC),
        cell_major(curv_root),
        directions.reshape(UNITS, OUTC),
    )
    return out.reshape(UNITS, 1, OUTC)


def solution(mesh):
    placed = (
        P(("wide", "narrow"), None, None, None),
        P(),
        P(),
        P(),
        P(),
        P(None, ("wide", "narrow")),
        P(("wide", "narrow")),
        P(),
        P(("wide", "narrow"), None, None, None),
        P(("wide", "narrow"), None, None),
    )
    return jax.shard_map(
        per_device,
        mesh=mesh,
        in_specs=placed,
        out_specs=P(("wide", "narrow"), None, None),
        check_vma=False,
    )
```

time: 110 us -> 80.2 us (0.73)
  matrix products: 18.7 us -> 0 us
  Pallas kernels: 82.5 us -> 77.2 us
  other arithmetic: 2.74 us -> 0 us
  local copies, waits for them, and re-layouts: 5.38 us -> 2.66 us
    conv_general_dilated x1 -> x0, matrix products: 18.7 us -> none  [features(): lax.conv_general_dilated(images.astype(F32), kernel, (1, 1), 'SAME', dime...]
    pallas_call x1, Pallas kernels: 82.5 us -> 77.2 us  [step(): pl.pallas_call(body, out_shape=jax.ShapeDtypeStruct((UNITS, OUTC), F32),...]
    unnamed x21 -> x1, local copies, waits for them, and re-layouts: 4.29 us -> 1.32 us
    convert_element_type x1 -> x0, other arithmetic: 1.5 us -> none  [features(): return normed.astype(BF16)]
    reduce_sum x1 -> x0, other arithmetic: 1.2 us -> none  [features(): variance = jnp.mean(jnp.square(mixed - average), axis=3, keepdims=True)]
where the time goes in v2:
time: 80.2 us; the launch traced here: 79.8 us
  Pallas kernels  77.2 us (96%)
  local copies, waits for them, and re-layouts  2.66 us (3%)
    pallas_call x1, Pallas kernels, step(): pl.pallas_call(body, out_shape=jax.ShapeDtypeStruct((UNITS, OUTC), F32),...  77.2 us

profile of v2, /device:TPU:1, one launch (start us, length us, event | category | flops | bytes accessed | tf_op | source)
XLA Modules:
  0.0 79.8 jit_solution(17803159827574153748)
XLA Ops:
  0.0 1.3 %copy.16 = f32[8,1,512]{2,0,1:T(8,128)} copy(f32[8,1,512]{2,1,0:T(1,128)} %param.19) | data formatting | bytes 32768
  1.3 77.2 %shard_map.100 = f32[8,512]{1,0:T(8,128)} custom-call(bf16[196,32,128]{2,1,0:T(8,128)(2,1)} %bitcast.30, f32[7,7,1024]{2,1,0:T(8,128)} %kernel_hbm.1, f32[1,1024]{1,0:T(1,128)} %bitcast.35, f32[1,1024]{1,0:T(1,128)} %bitcast.36, f32[1,1024]{1,0:T(1,128)} %bitcast.37, bf16[16,512]{1,0:T(8,128)(2,1)} %bitcast.34, bf16[1,8]{1,0:T(2,128)(2,1)} %bitcast.39, ...), custom_call_target="tpu_custom_call" | custom-call | tf_op jit(solution)/shard_map/pallas_call | solution.py:466
  78.5 1.3 %copy.13 = f32[8,1,512]{2,1,0:T(1,128)} copy(f32[8,1,512]{2,0,1:T(8,128)} %bitcast.32) | data formatting | bytes 32768 | tf_op jit(solution)/shard_map/reshape | solution.py:531

commit v3 on v2

--- a/solution.py
+++ b/solution.py
@@ -24,8 +24,7 @@
 ALL_CELLS = 1024 * CELLS
 UNITS = 8
 BLOCK = 64
-WROWS = 8 * BLOCK + 16
-DROWS = 4 * BLOCK
+CROWS = 4 * BLOCK
 TILE = 256
 PAIR = 2 * SIDE
 
@@ -74,10 +73,13 @@
     mixed,
     normed,
     curvature,
-    wz,
-    dz,
-    wbuf,
-    dbuf,
+    z_low,
+    z_high,
+    z_dir,
+    w_low,
+    w_high,
+    w_dir,
+    late,
     hidden,
     cell_out,
     cell_weight,
@@ -85,6 +87,7 @@
     pair_recv,
     slab_send,
     slab_recv,
+    kept,
     block_send,
     block_recv,
     row_send,
@@ -153,15 +156,17 @@
         pl.semaphore_signal(barrier, inc=1, device_id=group_of(k), device_id_type=MESH)
         pl.semaphore_signal(barrier, inc=1, device_id=plane_of(k), device_id_type=MESH)
 
-    wz[0, :, 0:512] = w_ref[...]
+    z_low[0] = w_ref[0:16, :]
+    z_high[0, :, 0:256] = w_ref[16:32, :]
     row8 = lax.broadcasted_iota(jnp.int32, (8, 8), 0)
     lane8 = lax.broadcasted_iota(jnp.int32, (8, 8), 1)
     line = jnp.broadcast_to(b_ref[...].astype(F32), (8, 8))
     column = jnp.sum(jnp.where(row8 == lane8, line, 0.0), axis=1, keepdims=True)
     column = jnp.broadcast_to(column, (8, 128))
-    wz[0, :, 512:640] = jnp.concatenate([column, column], axis=0).astype(BF16)
-    own = dir_ref[...]
-    dz[0] = jnp.concatenate([own[:, :256], own[:, 256:]], axis=0).astype(BF16)
+    z_high[0, :, 256:384] = jnp.concatenate([column, column], axis=0).astype(BF16)
+    own = dir_ref[:, 0, :]
+    z_dir[0] = jnp.concatenate([own[:, :128], own[:, 128:256]], axis=0).astype(BF16)
+    late[0, 0, 0, 0] = jnp.concatenate([own[:, 256:384], own[:, 384:]], axis=0).astype(BF16)
 
     def gather_z(buf, sem):
         for k in range(1, 8):
@@ -178,40 +183,40 @@
     def to_sibling(buf, off, sem):
         remote(buf.at[0, off], buf.at[1, off], sem, sibling).start()
 
-    def unpack_w():
-        raw = wz[...].astype(F32)
-        halves = (raw[:, :8, :512].reshape(BLOCK, 512), raw[:, 8:, :512].reshape(BLOCK, 512))
-        for k in range(8):
-            piece = halves[k // 4][:, (k % 4) * 128 : (k % 4 + 1) * 128]
-            wbuf[0, 0, 0, k * BLOCK : (k + 1) * BLOCK, :] = piece.astype(BF16)
-        bias = raw[:, :8, 512:].reshape(BLOCK, 128)
-        row_at = lax.broadcasted_iota(jnp.int32, (BLOCK, 128), 0)
-        lane_at = lax.broadcasted_iota(jnp.int32, (BLOCK, 128), 1) % BLOCK
-        total = jnp.sum(jnp.where(row_at == lane_at, bias, 0.0), axis=0, keepdims=True)
-        wbuf[0, 0, 0, 8 * BLOCK :, :] = jnp.broadcast_to(total, (16, 128)).astype(BF16)
-
-    def unpack_d():
-        raw = dz[...].astype(F32)
-        halves = (raw[:, :8].reshape(BLOCK, 256), raw[:, 8:].reshape(BLOCK, 256))
-        for k in range(4):
-            piece = halves[k // 2][:, (k % 2) * 128 : (k % 2 + 1) * 128]
-            dbuf[0, 0, 0, k * BLOCK : (k + 1) * BLOCK, :] = piece.astype(BF16)
-
-    def weight_tile(h, s):
+    def unpack(zbuf, buf):
+        raw = zbuf[...].astype(F32)
+        tiles = zbuf.shape[2] // 256 * 4 or 2
+        width = tiles * 64
+        halves = (raw[:, :8, :width].reshape(BLOCK, width), raw[:, 8:, :width].reshape(BLOCK, width))
+        for k in range(tiles):
+            lane = k * 128 % width
+            piece = halves[k // (tiles // 2)][:, lane : lane + 128]
+            buf[0, 0, 0, k * BLOCK : (k + 1) * BLOCK, :] = piece.astype(BF16)
+        if zbuf.shape[2] > 256:
+            bias = raw[:, :8, 256:].reshape(BLOCK, 128)
+            row_at = lax.broadcasted_iota(jnp.int32, (BLOCK, 128), 0)
+            lane_at = lax.broadcasted_iota(jnp.int32, (BLOCK, 128), 1) % BLOCK
+            total = jnp.sum(jnp.where(row_at == lane_at, bias, 0.0), axis=0, keepdims=True)
+            buf[0, 0, 0, CROWS:, :] = jnp.broadcast_to(total, (16, 128)).astype(BF16)
+
+    def chunk_tile(buf, h, s, tiles=4):
         return jnp.concatenate(
-            [wbuf[h, s, :, k * BLOCK : (k + 1) * BLOCK, :].reshape(TILE, 128) for k in range(8)], axis=1
+            [buf[h, s, :, k * BLOCK : (k + 1) * BLOCK, :].reshape(TILE, 128) for k in range(tiles)], axis=1
         )
 
+    def late_tile(h, s):
+        raw = late[h, :, s].astype(F32)
+        sides = [
+            jnp.concatenate([raw[kz, k2, lo : lo + 8] for k2 in range(4) for kz in range(8)], axis=0)
+            for lo in (0, 8)
+        ]
+        return jnp.concatenate(sides, axis=1).astype(BF16)
+
     def bias_tile(h, s):
-        rows = wbuf[h, s, :, 8 * BLOCK :, :].astype(F32)
+        rows = w_high[h, s, :, CROWS:, :].astype(F32)
         lane = lax.broadcasted_iota(jnp.int32, (16, 128), 1)
         lines = [jnp.where(lane < BLOCK, rows[2 * k], rows[2 * k + 1])[:1] for k in range(2)]
         return jnp.concatenate(lines, axis=1)
-
-    def direction_tile(h, s):
-        return jnp.concatenate(
-            [dbuf[h, s, :, k * BLOCK : (k + 1) * BLOCK, :].reshape(TILE, 128) for k in range(4)], axis=1
-        )
 
     def two_tiles(row, j):
         return jnp.where(
@@ -282,57 +287,89 @@
             pixels[2 * j, cells] = block[:, :8]
             pixels[2 * j + 1, cells] = block[:, 8:]
 
-    W, D = 0, 20
-    pl.semaphore_wait(barrier, 30)
-    gather_z(wz, W)
-    gather_z(dz, D)
+    chunks = ((z_low, w_low, 0), (z_high, w_high, 20), (z_dir, w_dir, 40))
+    LOW, HIGH, DIR = chunks
 
     def conv(first):
         conv_rows(first)
         norm_rows(first)
 
+    def after_z(chunk):
+        zbuf, buf, sem = chunk
+        arrived(sem, zbuf.at[pl.ds(1, 7)])
+        unpack(zbuf, buf)
+        gather_a2(buf, sem + 1)
+        if chunk is not DIR:
+            spread(buf, 1, 0, 1, sem + 2)
+            spread(buf, 3, 0, 1, sem + 3)
+
+    def after_a2(chunk):
+        _, buf, sem = chunk
+        arrived(sem + 1, buf.at[0, 0, pl.ds(1, 3)])
+        if chunk is DIR:
+            for k in (1, 3, 2):
+                spread(buf, k, 0, 4, sem + 1 + k)
+        else:
+            spread(buf, 1, 1, 3, sem + 4)
+            spread(buf, 3, 1, 3, sem + 5)
+        to_sibling(buf, 0, sem + 6)
+
+    def after_a3(chunk):
+        _, buf, sem = chunk
+        arrived(sem + 2, buf.at[0, 3, pl.ds(0, 1)])
+        arrived(sem + 4, buf.at[0, 3, pl.ds(1, 3)])
+        remote(buf.at[0, 3, pl.ds(0, 2)], buf.at[0, 2, pl.ds(0, 2)], sem + 10, along(1, 0, 0)).start()
+        arrived(sem + 3, buf.at[0, 1, pl.ds(0, 1)])
+        arrived(sem + 5, buf.at[0, 1, pl.ds(1, 3)])
+        remote(buf.at[0, 1, pl.ds(2, 2)], buf.at[0, 2, pl.ds(2, 2)], sem + 11, along(3, 0, 0)).start()
+        to_sibling(buf, 3, sem + 9)
+        to_sibling(buf, 1, sem + 7)
+
+    def after_forward(chunk):
+        _, buf, sem = chunk
+        arrived(sem + 10, buf.at[0, 2, pl.ds(0, 2)])
+        arrived(sem + 11, buf.at[0, 2, pl.ds(2, 2)])
+        to_sibling(buf, 2, sem + 8)
+
+    def from_sibling(chunk, off):
+        _, buf, sem = chunk
+        arrived(sem + 6 + off, buf.at[1, off])
+
+    def project(p, h, s):
+        weights = jnp.concatenate([chunk_tile(w_low, h, s), chunk_tile(w_high, h, s)], axis=1)
+        pre = lax.dot_general(
+            normed[...], weights, (((1,), (1,)), ((), ())), preferred_element_type=F32
+        )
+        hidden[:, p * TILE : (p + 1) * TILE] = gelu(pre + bias_tile(h, s)).astype(BF16)
+
+    places = [(0, 0), (1, 0), (0, 3), (1, 3), (0, 1), (1, 1), (0, 2), (1, 2)]
+
+    pl.semaphore_wait(barrier, 30)
+    L = 60
+    for k in range(1, 4):
+        remote(late.at[0, 0, 0, 0], late.at[0, 0, 0, 4 - k], L, along(0, k, 0)).start()
+    for zbuf, _, sem in chunks:
+        gather_z(zbuf, sem)
+
     conv(0)
     conv(2)
+    arrived(L, late.at[0, 0, 0, pl.ds(1, 3)])
+    for k in range(1, 4):
+        remote(late.at[0, 0, 0], late.at[0, 0, 4 - k], L + 1, along(k, 0, 0)).start()
     conv(4)
-
-    arrived(W, wz.at[pl.ds(1, 7)])
-    unpack_w()
-    gather_a2(wbuf, W + 1)
-    spread(wbuf, 1, 0, 1, W + 2)
-    spread(wbuf, 3, 0, 1, W + 3)
-    arrived(D, dz.at[pl.ds(1, 7)])
-    unpack_d()
-    gather_a2(dbuf, D + 1)
-
+    after_z(LOW)
+    after_z(HIGH)
+    arrived(L + 1, late.at[0, 0, pl.ds(1, 3)])
+    for k in (4, 3, 5, 2, 6, 1, 7):
+        remote(late.at[0, 0], late.at[0, 8 - k], L + 2, along(0, 0, k)).start()
     conv(6)
+    after_z(DIR)
     conv(8)
-
-    arrived(W + 1, wbuf.at[0, 0, pl.ds(1, 3)])
-    spread(wbuf, 1, 1, 3, W + 4)
-    spread(wbuf, 3, 1, 3, W + 5)
-    to_sibling(wbuf, 0, W + 6)
-
+    after_a2(LOW)
     conv(10)
-
-    arrived(D + 1, dbuf.at[0, 0, pl.ds(1, 3)])
-    to_sibling(dbuf, 0, D + 6)
-
+    after_a2(HIGH)
     conv(12)
-
-    for k in (1, 3, 2):
-        spread(dbuf, k, 0, 4, D + 1 + k)
-
-    def project(p, h, s):
-        pre = lax.dot_general(
-            normed[...], weight_tile(h, s), (((1,), (1,)), ((), ())), preferred_element_type=F32
-        )
-        hidden[:, p * TILE : (p + 1) * TILE] = gelu(pre + bias_tile(h, s)).astype(BF16)
-
-    places = [(0, 0), (1, 0), (0, 3), (1, 3), (0, 1), (1, 1), (0, 2), (1, 2)]
-
-    project(0, 0, 0)
-    arrived(W + 6, wbuf.at[1, 0])
-    project(1, 1, 0)
+    after_a2(DIR)
 
     loads[2].wait()
     for k in range(2):
@@ -341,34 +378,43 @@
         curvature[2 * k] = first
         curvature[2 * k + 1] = second
 
-    arrived(W + 2, wbuf.at[0, 3, pl.ds(0, 1)])
-    arrived(W + 4, wbuf.at[0, 3, pl.ds(1, 3)])
-    remote(wbuf.at[0, 3, pl.ds(0, 2)], wbuf.at[0, 2, pl.ds(0, 2)], W + 10, along(1, 0, 0)).start()
-    to_sibling(wbuf, 3, W + 9)
-    arrived(W + 3, wbuf.at[0, 1, pl.ds(0, 1)])
-    arrived(W + 5, wbuf.at[0, 1, pl.ds(1, 3)])
-    remote(wbuf.at[0, 1, pl.ds(2, 2)], wbuf.at[0, 2, pl.ds(2, 2)], W + 11, along(3, 0, 0)).start()
-    to_sibling(wbuf, 1, W + 7)
+    project(0, 0, 0)
+    after_a3(LOW)
+    from_sibling(LOW, 0)
+    from_sibling(HIGH, 0)
+    project(1, 1, 0)
+    after_a3(HIGH)
     project(2, 0, 3)
-    arrived(W + 9, wbuf.at[1, 3])
+    project(4, 0, 1)
+    arrived(L + 2, late.at[0, pl.ds(1, 7)])
+    remote(late.at[0], late.at[1], L + 3, sibling).start()
+    for k in (1, 3, 2):
+        arrived(40 + 1 + k, w_dir.at[0, 4 - k])
+        to_sibling(w_dir, 4 - k, 40 + 6 + 4 - k)
+    after_forward(LOW)
+    for off in (3, 1):
+        from_sibling(LOW, off)
+        from_sibling(HIGH, off)
     project(3, 1, 3)
-    project(4, 0, 1)
-    arrived(W + 7, wbuf.at[1, 1])
     project(5, 1, 1)
-    arrived(W + 10, wbuf.at[0, 2, pl.ds(0, 2)])
-    arrived(W + 11, wbuf.at[0, 2, pl.ds(2, 2)])
-    to_sibling(wbuf, 2, W + 8)
+
+    def direction_tile(h, s):
+        return jnp.concatenate([chunk_tile(w_dir, h, s, 2), late_tile(h, s)], axis=1)
+
+    def partial(lo, hi):
+        directions = jnp.concatenate([direction_tile(h, s) for h, s in places[lo:hi]], axis=0)
+        return jnp.dot(hidden[:, lo * TILE : hi * TILE], directions, preferred_element_type=F32)
+
+    after_forward(HIGH)
+    for off in range(4):
+        from_sibling(DIR, off)
+    arrived(L + 3, late.at[1])
+    cell_out[...] = partial(0, 6)
     project(6, 0, 2)
-    for k in (1, 3, 2):
-        arrived(D + 1 + k, dbuf.at[0, 4 - k])
-        to_sibling(dbuf, 4 - k, D + 6 + 4 - k)
-    arrived(W + 8, wbuf.at[1, 2])
+    from_sibling(LOW, 2)
+    from_sibling(HIGH, 2)
     project(7, 1, 2)
-    for off in range(4):
-        arrived(D + 6 + off, dbuf.at[1, off])
-
-    directions = jnp.concatenate([direction_tile(h, s) for h, s in places], axis=0)
-    cell_out[...] = jnp.dot(hidden[...], directions, preferred_element_type=F32)
+    cell_out[...] += partial(6, 8)
 
     scale = gamma_ref[...] * gamma_ref[...]
     for k in range(4):
@@ -389,75 +435,92 @@
             preferred_element_type=F32,
         )
 
-    R = 40
+    R = 64
     for off in (2, 1, 3, 0):
         pair_send[off] = product(1, off).astype(BF16)
         remote(pair_send.at[off], pair_recv.at[off], R + off, sibling).start()
+    onward, home = pl.ds(1, 3), pl.ds(0, 1)
     for off in (2, 1, 3):
         part = product(0, off)
         arrived(R + off, pair_recv.at[off])
-        slab_send[off - 1] = (part + pair_recv[off].astype(F32)).astype(BF16)
-        remote(slab_send.at[off - 1], slab_recv.at[off - 1], R + 3 + off, along(off, 0, 0)).start()
+        part = part + pair_recv[off].astype(F32)
+        slab_send[off - 1] = part.reshape(4, BLOCK, OUTC).astype(BF16)
+        place = slab_recv.at[off - 1, onward]
+        remote(slab_send.at[off - 1, onward], place, R + 3 + off, along(off, 0, 0)).start()
+    for off in (2, 1, 3):
+        place = slab_recv.at[off - 1, home]
+        remote(slab_send.at[off - 1, home], place, R + 6 + off, along(off, 0, 0)).start()
     part = product(0, 0)
     arrived(R, pair_recv.at[0])
-    part = part + pair_recv[0].astype(F32)
+    kept[...] = (part + pair_recv[0].astype(F32)).reshape(4, BLOCK, OUTC)
     for off in (1, 3, 2):
-        arrived(R + 3 + off, slab_recv.at[off - 1])
-        part = part + slab_recv[off - 1].astype(F32)
-    blocks = part.reshape(4, BLOCK, OUTC)
-    for off in (2, 1, 3):
-        block_send[off - 1] = blocks[off].astype(BF16)
-        remote(block_send.at[off - 1], block_recv.at[off - 1], R + 6 + off, along(0, off, 0)).start()
-    part = blocks[0]
+        arrived(R + 3 + off, slab_recv.at[off - 1, onward])
+    for k in (2, 1, 3):
+        block = kept[k]
+        for off in (1, 2, 3):
+            block = block + slab_recv[off - 1, k].astype(F32)
+        block_send[k - 1] = block.astype(BF16)
+        remote(block_send.at[k - 1], block_recv.at[k - 1], R + 9 + k, along(0, k, 0)).start()
+    block = kept[0]
     for off in (1, 3, 2):
-        arrived(R + 6 + off, block_recv.at[off - 1])
-        part = part + block_recv[off - 1].astype(F32)
-    rows = part.reshape(8, UNITS, OUTC)
+        arrived(R + 6 + off, slab_recv.at[off - 1, home])
+        block = block + slab_recv[off - 1, 0].astype(F32)
+    for off in (1, 3, 2):
+        arrived(R + 9 + off, block_recv.at[off - 1])
+        block = block + block_recv[off - 1].astype(F32)
+    rows = block.reshape(8, UNITS, OUTC)
     for k in (4, 3, 5, 2, 6, 1, 7):
         row_send[k - 1] = jnp.concatenate([rows[k, :, :256], rows[k, :, 256:]], axis=0).astype(BF16)
-        remote(row_send.at[k - 1], row_recv.at[k - 1], R + 10, along(0, 0, k)).start()
-    arrived(R + 10, row_recv)
+        remote(row_send.at[k - 1], row_recv.at[k - 1], R + 13, along(0, 0, k)).start()
+    arrived(R + 13, row_recv)
     others = jnp.sum(row_recv[...].astype(F32), axis=0)
     summed = rows[0] + jnp.concatenate([others[:8], others[8:]], axis=1)
 
-    estimate = dir_ref[...]
+    N = R + 14
+    estimate = dir_ref[:, 0, :]
     fresh = estimate + (1.0 - damping) * estimate - summed * (1.0 / (scale_coef * ALL_CELLS))
     fresh_part = jnp.sum(fresh * fresh, axis=(0, 1), keepdims=True)
     direction_part = jnp.sum(estimate * estimate, axis=(0, 1), keepdims=True)
     row = lax.broadcasted_iota(jnp.int32, (8, 128), 0)
     sums[...] = jnp.where(row < 4, fresh_part, direction_part)
     for k in range(1, 16):
-        remote(sums, sums_recv.at[k - 1], R + 11, group_of(k)).start()
-    arrived(R + 11, sums_recv)
+        remote(sums, sums_recv.at[k - 1], N, group_of(k)).start()
+    arrived(N, sums_recv)
     wide_sums[...] = sums[...] + jnp.sum(sums_recv[...], axis=0)
     for k in range(1, 16):
-        remote(wide_sums, wide_recv.at[k - 1], R + 12, plane_of(k)).start()
-    arrived(R + 12, wide_recv)
+        remote(wide_sums, wide_recv.at[k - 1], N + 1, plane_of(k)).start()
+    arrived(N + 1, wide_recv)
     sq = wide_sums[...] + jnp.sum(wide_recv[...], axis=0)
     fresh_sq = sq[0:1, 0:1]
     direction_sq = sq[4:5, 0:1]
     factor = jnp.minimum(1.0, clip_ratio * jnp.sqrt(direction_sq / (fresh_sq + 1e-06)))
     out_ref[...] = fresh * factor
 
-    for buf, zbuf, base in ((wbuf, wz, W), (dbuf, dz, D)):
+    for zbuf, buf, base in chunks:
         left(base, zbuf.at[pl.ds(1, 7)])
         left(base + 1, buf.at[0, 0, pl.ds(1, 3)])
         for off in range(4):
             left(base + 6 + off, buf.at[0, off])
-    for k in range(2):
-        left(W + 2 + k, wbuf.at[0, 0, pl.ds(0, 1)])
-        left(W + 4 + k, wbuf.at[0, 0, pl.ds(1, 3)])
-        left(W + 10 + k, wbuf.at[0, 0, pl.ds(0, 2)])
+    for _, buf, base in (LOW, HIGH):
+        for k in range(2):
+            left(base + 2 + k, buf.at[0, 0, pl.ds(0, 1)])
+            left(base + 4 + k, buf.at[0, 0, pl.ds(1, 3)])
+            left(base + 10 + k, buf.at[0, 0, pl.ds(0, 2)])
     for k in (1, 3, 2):
-        left(D + 1 + k, dbuf.at[0, 0])
+        left(40 + 1 + k, w_dir.at[0, 0])
+    left(L, late.at[0, 0, 0, pl.ds(1, 3)])
+    left(L + 1, late.at[0, 0, pl.ds(1, 3)])
+    left(L + 2, late.at[0, pl.ds(1, 7)])
+    left(L + 3, late.at[0])
     for off in range(4):
         left(R + off, pair_send.at[off])
     for off in range(1, 4):
-        left(R + 3 + off, slab_send.at[off - 1])
-        left(R + 6 + off, block_send.at[off - 1])
-    left(R + 10, row_recv)
-    left(R + 11, sums_recv)
-    left(R + 12, wide_recv)
+        left(R + 3 + off, slab_send.at[off - 1, onward])
+        left(R + 6 + off, slab_send.at[off - 1, home])
+        left(R + 9 + off, block_send.at[off - 1])
+    left(R + 13, row_recv)
+    left(N, sums_recv)
+    left(N + 1, wide_recv)
 
 
 def step(*operands):
@@ -478,17 +541,21 @@
             pltpu.VMEM((4, PAIR, 8, 128), F32),
             pltpu.VMEM((ROWS, CH), BF16),
             pltpu.VMEM((4, CELLS // 2, 8, 128), F32),
-            pltpu.VMEM((8, 16, 640), BF16),
             pltpu.VMEM((8, 16, 256), BF16),
-            pltpu.VMEM((2, 4, 4, WROWS, 128), BF16),
-            pltpu.VMEM((2, 4, 4, DROWS, 128), BF16),
+            pltpu.VMEM((8, 16, 384), BF16),
+            pltpu.VMEM((8, 16, 128), BF16),
+            pltpu.VMEM((2, 4, 4, CROWS, 128), BF16),
+            pltpu.VMEM((2, 4, 4, CROWS + 16, 128), BF16),
+            pltpu.VMEM((2, 4, 4, CROWS // 2, 128), BF16),
+            pltpu.VMEM((2, 8, 4, 4, 16, 128), BF16),
             pltpu.VMEM((ROWS, HID), BF16),
             pltpu.VMEM((ROWS, OUTC), F32),
             pltpu.VMEM((ROWS, OUTC), BF16),
             pltpu.VMEM((4, TILE, OUTC), BF16),
             pltpu.VMEM((4, TILE, OUTC), BF16),
-            pltpu.VMEM((3, TILE, OUTC), BF16),
-            pltpu.VMEM((3, TILE, OUTC), BF16),
+            pltpu.VMEM((3, 4, BLOCK, OUTC), BF16),
+            pltpu.VMEM((3, 4, BLOCK, OUTC), BF16),
+            pltpu.VMEM((4, BLOCK, OUTC), F32),
             pltpu.VMEM((3, BLOCK, OUTC), BF16),
             pltpu.VMEM((3, BLOCK, OUTC), BF16),
             pltpu.VMEM((7, 16, 256), BF16),
@@ -497,8 +564,8 @@
             pltpu.VMEM((15, 8, 128), F32),
             pltpu.VMEM((8, 128), F32),
             pltpu.VMEM((15, 8, 128), F32),
-            pltpu.SemaphoreType.DMA((60,)),
-            pltpu.SemaphoreType.DMA((60,)),
+            pltpu.SemaphoreType.DMA((96,)),
+            pltpu.SemaphoreType.DMA((96,)),
             pltpu.SemaphoreType.DMA((3,)),
         ],
         compiler_params=pltpu.CompilerParams(
@@ -522,11 +589,11 @@
         dw_bias.reshape(1, CH),
         ln_gain.reshape(1, CH),
         ln_bias.reshape(1, CH),
-        w_in.T.reshape(UNITS, 2, 512).transpose(1, 0, 2).reshape(16, 512),
+        w_in.T.reshape(UNITS, 4, 256).transpose(1, 0, 2).reshape(32, 256),
         b_in.reshape(1, UNITS),
         gamma.reshape(1, OUTC),
         cell_major(curv_root),
-        directions.reshape(UNITS, OUTC),
+        directions,
     )
     return out.reshape(UNITS, 1, OUTC)
 

time: 80.2 us -> 71.7 us (0.89)
  Pallas kernels: 77.2 us -> 70.1 us
  local copies, waits for them, and re-layouts: 2.66 us -> 1.34 us
    pallas_call x1, Pallas kernels: 77.2 us -> 70.1 us  [step(): pl.pallas_call(body, out_shape=jax.ShapeDtypeStruct((UNITS, OUTC), F32),...]
    unnamed x1 -> x0, local copies, waits for them, and re-layouts: 1.32 us -> none
where the time goes in v3:
time: 71.7 us; the launch traced here: 71.4 us
  Pallas kernels  70.1 us (98%)
  local copies, waits for them, and re-layouts  1.34 us (2%)
    pallas_call x1, Pallas kernels, step(): pl.pallas_call(body, out_shape=jax.ShapeDtypeStruct((UNITS, OUTC), F32),...  70.1 us

profile of v3, /device:TPU:1, one launch (start us, length us, event | category | flops | bytes accessed | tf_op | source)
XLA Modules:
  0.0 71.4 jit_solution(2686978216076176325)
XLA Ops:
  0.0 70.1 %shard_map.100 = f32[8,512]{1,0:T(8,128)} custom-call(bf16[196,32,128]{2,1,0:T(8,128)(2,1)} %bitcast.27, f32[7,7,1024]{2,1,0:T(8,128)} %kernel_hbm.1, f32[1,1024]{1,0:T(1,128)} %bitcast.31, f32[1,1024]{1,0:T(1,128)} %bitcast.32, f32[1,1024]{1,0:T(1,128)} %bitcast.33, bf16[32,256]{1,0:T(8,128)(2,1)} %bitcast.30, bf16[1,8]{1,0:T(2,128)(2,1)} %bitcast.35, ...), custom_call_target="tpu_custom_call" | custom-call | tf_op jit(solution)/shard_map/pallas_call | solution.py:529
  70.1 1.3 %copy.13 = f32[8,1,512]{2,1,0:T(1,128)} copy(f32[8,1,512]{2,0,1:T(8,128)} %bitcast.29) | data formatting | bytes 32768 | tf_op jit(solution)/shard_map/reshape | solution.py:598

commit v4 on v3

--- a/solution.py
+++ b/solution.py
@@ -26,6 +26,8 @@
 BLOCK = 64
 CROWS = 4 * BLOCK
 TILE = 256
+FAR_FIRST = (8, 7, 9, 6, 10, 5, 11, 4, 12, 3, 13, 2, 14, 1, 15)
+PLANE_FAR_FIRST = (10, 9, 11, 6, 14, 5, 7, 13, 15, 2, 8, 1, 3, 4, 12)
 PAIR = 2 * SIDE
 
 
@@ -152,7 +154,7 @@
         pltpu.make_async_copy(ref, ref, send.at[sem]).wait()
 
     barrier = pltpu.get_barrier_semaphore()
-    for k in range(1, 16):
+    for k in FAR_FIRST:
         pl.semaphore_signal(barrier, inc=1, device_id=group_of(k), device_id_type=MESH)
         pl.semaphore_signal(barrier, inc=1, device_id=plane_of(k), device_id_type=MESH)
 
@@ -169,11 +171,11 @@
     late[0, 0, 0, 0] = jnp.concatenate([own[:, 256:384], own[:, 384:]], axis=0).astype(BF16)
 
     def gather_z(buf, sem):
-        for k in range(1, 8):
+        for k in (4, 3, 5, 2, 6, 1, 7):
             remote(buf.at[0], buf.at[8 - k], sem, along(0, 0, k)).start()
 
     def gather_a2(buf, sem):
-        for k in range(1, 4):
+        for k in (2, 1, 3):
             remote(buf.at[0, 0, 0], buf.at[0, 0, 4 - k], sem, along(0, k, 0)).start()
 
     def spread(buf, k, lo, count, sem):
@@ -263,30 +265,6 @@
                     values[k].reshape(PAIR * IMGS, 128).astype(BF16)
                 )
 
-    loads[1].wait()
-
-    @pl.loop(0, KER)
-    def _(kh):
-        for kw in range(KER):
-            line = kernel[kh, kw : kw + 1, :]
-            for j in range(4):
-                taps[j, kh * KER + kw] = two_tiles(line, j)
-
-    for j in range(4):
-        scales[0, j] = two_tiles(dw_bias_ref[...], j)
-        scales[1, j] = two_tiles(gain_ref[...], j)
-        scales[2, j] = two_tiles(ln_bias_ref[...], j)
-
-    loads[0].wait()
-
-    @pl.loop(0, SIDE)
-    def _(r):
-        cells = pl.ds(r * SIDE, SIDE)
-        for j in range(2):
-            block = images[cells, 16 * j : 16 * j + 16, :].astype(F32)
-            pixels[2 * j, cells] = block[:, :8]
-            pixels[2 * j + 1, cells] = block[:, 8:]
-
     chunks = ((z_low, w_low, 0), (z_high, w_high, 20), (z_dir, w_dir, 40))
     LOW, HIGH, DIR = chunks
 
@@ -350,6 +328,30 @@
         remote(late.at[0, 0, 0, 0], late.at[0, 0, 0, 4 - k], L, along(0, k, 0)).start()
     for zbuf, _, sem in chunks:
         gather_z(zbuf, sem)
+
+    loads[1].wait()
+
+    @pl.loop(0, KER)
+    def _(kh):
+        for kw in range(KER):
+            line = kernel[kh, kw : kw + 1, :]
+            for j in range(4):
+                taps[j, kh * KER + kw] = two_tiles(line, j)
+
+    for j in range(4):
+        scales[0, j] = two_tiles(dw_bias_ref[...], j)
+        scales[1, j] = two_tiles(gain_ref[...], j)
+        scales[2, j] = two_tiles(ln_bias_ref[...], j)
+
+    loads[0].wait()
+
+    @pl.loop(0, SIDE)
+    def _(r):
+        cells = pl.ds(r * SIDE, SIDE)
+        for j in range(2):
+            block = images[cells, 16 * j : 16 * j + 16, :].astype(F32)
+            pixels[2 * j, cells] = block[:, :8]
+            pixels[2 * j + 1, cells] = block[:, 8:]
 
     conv(0)
     conv(2)
@@ -483,11 +485,11 @@
     direction_part = jnp.sum(estimate * estimate, axis=(0, 1), keepdims=True)
     row = lax.broadcasted_iota(jnp.int32, (8, 128), 0)
     sums[...] = jnp.where(row < 4, fresh_part, direction_part)
-    for k in range(1, 16):
+    for k in FAR_FIRST:
         remote(sums, sums_recv.at[k - 1], N, group_of(k)).start()
     arrived(N, sums_recv)
     wide_sums[...] = sums[...] + jnp.sum(sums_recv[...], axis=0)
-    for k in range(1, 16):
+    for k in PLANE_FAR_FIRST:
         remote(wide_sums, wide_recv.at[k - 1], N + 1, plane_of(k)).start()
     arrived(N + 1, wide_recv)
     sq = wide_sums[...] + jnp.sum(wide_recv[...], axis=0)

time: 71.7 us -> 71.4 us (level)
  no operation moved by 1% of the time
where the time goes in v4:
time: 71.4 us; the launch traced here: 71.1 us
  Pallas kernels  69.8 us (98%)
  local copies, waits for them, and re-layouts  1.34 us (2%)
    pallas_call x1, Pallas kernels, step(): pl.pallas_call(body, out_shape=jax.ShapeDtypeStruct((UNITS, OUTC), F32),...  69.8 us

profile of v4, /device:TPU:1, one launch (start us, length us, event | category | flops | bytes accessed | tf_op | source)
XLA Modules:
  0.0 71.1 jit_solution(8227469016547580910)
XLA Ops:
  0.0 69.8 %shard_map.100 = f32[8,512]{1,0:T(8,128)} custom-call(bf16[196,32,128]{2,1,0:T(8,128)(2,1)} %bitcast.27, f32[7,7,1024]{2,1,0:T(8,128)} %kernel_hbm.1, f32[1,1024]{1,0:T(1,128)} %bitcast.31, f32[1,1024]{1,0:T(1,128)} %bitcast.32, f32[1,1024]{1,0:T(1,128)} %bitcast.33, bf16[32,256]{1,0:T(8,128)(2,1)} %bitcast.30, bf16[1,8]{1,0:T(2,128)(2,1)} %bitcast.35, ...), custom_call_target="tpu_custom_call" | custom-call | tf_op jit(solution)/shard_map/pallas_call | solution.py:531
  69.8 1.3 %copy.13 = f32[8,1,512]{2,1,0:T(1,128)} copy(f32[8,1,512]{2,0,1:T(8,128)} %bitcast.29) | data formatting | bytes 32768 | tf_op jit(solution)/shard_map/reshape | solution.py:600

commit v5 on v4

--- a/solution.py
+++ b/solution.py
@@ -411,12 +411,12 @@
     for off in range(4):
         from_sibling(DIR, off)
     arrived(L + 3, late.at[1])
-    cell_out[...] = partial(0, 6)
     project(6, 0, 2)
+    cell_out[...] = partial(0, 7)
     from_sibling(LOW, 2)
     from_sibling(HIGH, 2)
     project(7, 1, 2)
-    cell_out[...] += partial(6, 8)
+    cell_out[...] += partial(7, 8)
 
     scale = gamma_ref[...] * gamma_ref[...]
     for k in range(4):

time: 71.4 us -> 71.4 us (level)
  no operation moved by 1% of the time
where the time goes in v5:
time: 71.4 us; the launch traced here: 71.1 us
  Pallas kernels  69.8 us (98%)
  local copies, waits for them, and re-layouts  1.34 us (2%)
    pallas_call x1, Pallas kernels, step(): pl.pallas_call(body, out_shape=jax.ShapeDtypeStruct((UNITS, OUTC), F32),...  69.8 us

profile of v5, /device:TPU:1, one launch (start us, length us, event | category | flops | bytes accessed | tf_op | source)
XLA Modules:
  0.0 71.1 jit_solution(2661556526866136961)
XLA Ops:
  0.0 69.8 %shard_map.100 = f32[8,512]{1,0:T(8,128)} custom-call(bf16[196,32,128]{2,1,0:T(8,128)(2,1)} %bitcast.27, f32[7,7,1024]{2,1,0:T(8,128)} %kernel_hbm.1, f32[1,1024]{1,0:T(1,128)} %bitcast.31, f32[1,1024]{1,0:T(1,128)} %bitcast.32, f32[1,1024]{1,0:T(1,128)} %bitcast.33, bf16[32,256]{1,0:T(8,128)(2,1)} %bitcast.30, bf16[1,8]{1,0:T(2,128)(2,1)} %bitcast.35, ...), custom_call_target="tpu_custom_call" | custom-call | tf_op jit(solution)/shard_map/pallas_call | solution.py:531
  69.8 1.3 %copy.13 = f32[8,1,512]{2,1,0:T(1,128)} copy(f32[8,1,512]{2,0,1:T(8,128)} %bitcast.29) | data formatting | bytes 32768 | tf_op jit(solution)/shard_map/reshape | solution.py:600
